TPU v7x, 32 devices: a whole 2x2x4 slice. The times are simulated.
32 devices in a mesh: row: 4 (over z), slab: 4 (over y, x), rep: 2 (over core).
Axes of the slice: x: 2, y: 2, z: 4, core: 2. Of those that a mesh axis runs over, the one named last changes fastest.
Arguments:
- t2_stored: float32 [2048, 40960], P('row', ('slab', 'rep')), may hold values from -6 to 6
- v_slab: float32 [1536, 40960], P('rep', 'slab'), may hold values from -0.03125 to 0.03125
- block_source: int32 [320], replicated, may hold values from 0 to 319, as said below
- r_in: float32 [2048, 1536], P(('row', 'slab'), 'rep'), may hold values from -6 to 6
Outputs:
- r_out: float32 [2048, 1536], P(('row', 'slab'), 'rep')
Inputs may be any that keep to these rules, and one draw needn't show every extreme that they name: block_source is a permutation of the 320 stored blocks. Slab index t owns the blocks k with k // 80 == t; stored block q lies on the device of slab and rep numbered q // 40. Every such device stores either none or exactly 10 blocks owned by any one slab index, and the slab indices it stores blocks for form a run of 4 consecutive indices counted modulo the slab axis.
All inputs are finite; a program needn't handle non-finite values.
Results may differ from a plain program's by a relative error of at most 0.000084.
Values sent between devices are 32-bit elements; how exact they have to be, the bound alone decides.
No kernel may reach another device: no remote copies, remote signals or barrier semaphores. Data moves between devices by JAX's collectives and lax.ppermute only.
A program may use at most 128 MiB of HBM per device.

v0:
```python
import jax
import jax.numpy as jnp
from jax import lax
from jax.sharding import PartitionSpec as P

BLK = 128


def block_maps(block_source, nblk_total, stored, blk_dev):
    indices = jnp.arange(nblk_total, dtype=jnp.int32)
    matches = block_source[None, :] == indices[:, None]
    position = jnp.sum(jnp.where(matches, indices[None, :], 0), axis=1)
    owner = position // blk_dev
    holder = indices // stored
    earlier = (
        (holder[None, :] == holder[:, None])
        & (owner[None, :] == owner[:, None])
        & (indices[None, :] < indices[:, None])
    )
    slot_rank = jnp.sum(earlier.astype(jnp.int32), axis=1)
    return (owner, slot_rank)


def per_device(t2_stored, v_slab, block_source, r_in):
    slab_count = lax.axis_size("slab")
    rep_count = lax.axis_size("rep")
    slab_index = lax.axis_index("slab")
    rep_index = lax.axis_index("rep")
    row_count = t2_stored.shape[0]
    stored = t2_stored.shape[1] // BLK
    blk_dev = v_slab.shape[1] // BLK
    nblk_total = blk_dev * slab_count
    capacity = max(2, stored // slab_count)
    owner, slot_rank = block_maps(block_source, nblk_total, stored, blk_dev)
    local_ids = slab_index * blk_dev + jnp.arange(blk_dev, dtype=jnp.int32)
    stored_ids = jnp.take(block_source, local_ids)
    source_holder = stored_ids // stored
    source_rank = jnp.take(slot_rank, stored_ids)
    own_blocks = (slab_index * rep_count + rep_index) * stored + jnp.arange(stored, dtype=jnp.int32)
    owners_here = jnp.take(owner, own_blocks)
    ranks_here = jnp.take(slot_rank, own_blocks)
    wanted = (
        owners_here[None, None, :] == jnp.arange(slab_count, dtype=jnp.int32)[:, None, None]
    ) & (ranks_here[None, None, :] == jnp.arange(capacity, dtype=jnp.int32)[None, :, None])
    chosen = jnp.sum(
        jnp.where(wanted, jnp.arange(stored, dtype=jnp.int32)[None, None, :], 0), axis=2
    )
    filled = jnp.any(wanted, axis=2)
    blocked = t2_stored.reshape(row_count, stored, BLK)
    picked = jnp.take(blocked, chosen.reshape(-1), axis=1)
    outgoing = jnp.where(filled.reshape(1, -1, 1), picked, 0.0).reshape(
        row_count, slab_count, capacity, BLK
    )
    arrived = lax.all_to_all(outgoing, "slab", split_axis=1, concat_axis=1, tiled=True)
    copies = lax.all_gather(arrived, "rep", axis=1, tiled=True)
    src_slab = source_holder // rep_count
    src_rep = source_holder % rep_count
    slot_ids = (src_rep * slab_count + src_slab) * capacity + source_rank
    ordered = jnp.take(copies.reshape(row_count, -1, BLK), slot_ids, axis=1).reshape(
        row_count, blk_dev * BLK
    )
    partial_value = lax.dot_general(
        ordered,
        v_slab,
        (((1,), (1,)), ((), ())),
        precision=lax.Precision.HIGHEST,
        preferred_element_type=jnp.float32,
    )
    portion = lax.psum_scatter(partial_value, "slab", scatter_dimension=0, tiled=True)
    return r_in + portion


def solution(mesh):
    in_specs = (P("row", ("slab", "rep")), P("rep", "slab"), P(), P(("row", "slab"), "rep"))
    out_specs = P(("row", "slab"), "rep")
    return jax.shard_map(
        per_device, mesh=mesh, in_specs=in_specs, out_specs=out_specs, check_vma=False
    )
```

profile of v0, /device:TPU:0, one launch (start us, length us, event | category | flops | bytes accessed | tf_op | source)
XLA Modules:
  0.0 401.2 jit_solution(6294258827936474751)
XLA Ops:
  6.5 0.0 all-gather.2.cloned.1.call-start
  6.6 0.8 select_reduce_fusion
  7.4 0.3 convert_reduce_fusion
  7.7 0.8 gather_fusion.4
  8.5 0.8 gather_fusion.5
  9.3 0.3 fusion.1
  9.6 0.1 copy.14
  9.7 0.3 and_reduce_fusion
  9.9 0.1 reshape.162
  10.0 11.4 %copy.13 = f32[512,5120]{0,1:T(8,128)} copy(f32[512,5120]{1,0:T(8,128)} %param.8) | data formatting | bytes 20971520 | tf_op args[0]
  21.4 11.3 %copy.15 = f32[512,40,128]{2,0,1:T(8,128)} copy(f32[512,40,128]{0,2,1:T(8,128)} %bitcast.16) | data formatting | bytes 20971520 | tf_op jit(solution)/shard_map/reshape | solution.py:49
  32.8 0.1 copy.12
  32.9 0.1 copy.11
  33.0 10.9 %gather_fusion = f32[40,512,128]{2,1,0:T(8,128)} fusion(f32[512,40,128]{2,0,1:T(8,128)} %copy.15, s32[1024]{0:T(1024)S(1)} %pad_clamp_fusion.1), kind=kCustom, calls=%fused_computation.4 | custom fusion | bytes 20971680 | tf_op jit(solution)/shard_map/jit(_take)/gather | solution.py:50
  43.9 6.3 %select_select_fusion = f32[512,4,10,128]{3,0,2,1:T(8,128)S(1)} fusion(f32[512,4,10,128]{3,0,2,1:T(8,128)} %bitcast.15, pred[4,10]{1,0:T(4,128)(4,1)S(1)} %copy.12, pred[4,10]{1,0:T(4,128)(4,1)S(1)} %copy.11), kind=kLoop, calls=%fused_computation.7 | loop fusion | flops 5242880 | bytes 20971600 | tf_op jit(solution)/shard_map/jit(_where)/select_n | solution.py:51
  50.2 120.8 %all_to_all.5 = f32[512,4,10,128]{3,0,2,1:T(8,128)} all-to-all(f32[512,4,10,128]{3,0,2,1:T(8,128)S(1)} %select_select_fusion), channel_id=1, replica_groups=mesh['row'=4,'slab'=4,'rep'=2] {'slab'}, dimensions={1} | all-to-all | bytes 20971520 | tf_op jit(solution)/shard_map/all_to_all | solution.py:54
  171.0 0.0 copy-start
  171.0 0.0 all-gather.2.cloned.1.call-update
  171.0 0.0 reduce-scatter.2.cloned.1.call-start
  171.1 0.6 copy-done
  171.7 1.3 gather_fusion.2
  173.0 1.3 gather_fusion.3
  174.3 0.1 broadcast_bitcast_fusion
  174.4 32.5 %all-gather.2.cloned.1.call-done = f32[512,8,10,128]{3,0,2,1:T(8,128)} async-done(((f32[512,4,10,128]{3,0,2,1:T(8,128)}), f32[512,8,10,128]{3,0,2,1:T(8,128)}) %all-gather.2.cloned.1.call-update) | async-done | bytes 20971536 | tf_op jit(solution)/shard_map/all_gather | solution.py:55
  206.9 17.0 %gather_fusion.1 = f32[80,512,128]{2,1,0:T(8,128)} fusion(f32[512,80,128]{2,0,1:T(8,128)} %bitcast.17, s32[1024]{0:T(1024)S(1)} %pad_clamp_fusion), kind=kCustom, calls=%fused_computation.5 | custom fusion | bytes 41943360 | tf_op jit(solution)/shard_map/jit(_take)/gather | solution.py:59
  224.0 21.3 %copy.16 = f32[512,80,128]{0,2,1:T(8,128)} copy(f32[512,80,128]{2,0,1:T(8,128)} %bitcast.14) | data formatting | bytes 41943040 | tf_op jit(solution)/shard_map/jit(_take)/gather | solution.py:59
  245.3 10.1 %bitcast_select_fusion = f32[512,10240]{0,1:T(8,128)S(1)} fusion(f32[512,80,128]{0,2,1:T(8,128)} %copy.16, pred[10240]{0:T(1024)(128)(4,1)S(1)} %broadcast_bitcast_fusion), kind=kLoop, calls=%fused_computation.6 | loop fusion | flops 5242880 | bytes 41953280 | tf_op jit(solution)/shard_map/jit(_take)/select_n | solution.py:59
  255.4 0.0 copy-start.1
  255.4 104.9 %fusion.10 = f32[512,768]{1,0:T(8,128)} fusion(f32[512,10240]{0,1:T(8,128)S(1)} %bitcast_select_fusion, f32[768,10240]{1,0:T(8,128)} %param.9), kind=kOutput, calls=%fused_computation.58 | convolution fusion | flops 48318382080 | bytes 54001664 | tf_op jit(solution)/shard_map/dot_general | solution.py:62
  360.3 0.0 reduce-scatter.2.cloned.1.call-update
  360.3 32.3 %reduce-scatter.2.cloned.1.call-done = f32[128,768]{1,0:T(8,128)} async-done(((f32[512,768]{1,0:T(8,128)}), f32[128,768]{1,0:T(8,128)}) %reduce-scatter.2.cloned.1.call-update) | async-done | bytes 393232 | tf_op jit(solution)/shard_map/reduce_scatter | solution.py:69
  392.6 0.0 copy-done.1
  392.6 1.8 add.108
  (16 shorter events, 0.1 us)
Async XLA Ops:
  6.5 200.4 %all-gather.2.cloned.1.call-start = ((), (), s32[]{:S(2)}) async-start(), calls=%async_computation.2 | async-start | bytes 31457280 | tf_op jit(solution)/shard_map/all_gather | solution.py:55
  171.0 0.7 copy-start
  171.0 221.5 %reduce-scatter.2.cloned.1.call-start = ((), (), s32[]{:S(2)}) async-start(), calls=%async_computation.3 | async-start | bytes 1966080 | tf_op jit(solution)/shard_map/reduce_scatter | solution.py:69
  255.4 137.2 %copy-start.1 = (f32[128,768]{1,0:T(8,128)S(1)}, f32[128,768]{1,0:T(8,128)}, u32[]{:S(2)}) copy-start(f32[128,768]{1,0:T(8,128)} %param.11) | copy-start | bytes 1179652
Sparse Core Ops, SparseCore 0:
  171.2 35.7 all-gather.1
  360.4 32.1 reduce-scatter.1
where the time goes:
time: 402 us; the launch traced here: 401 us
  blocking collectives  121 us (30%)
  matrix products  105 us (26%)
  local copies, waits for them, and re-layouts  77.2 us (19%)
  waiting for transfers between devices  64.9 us (16%)
  other arithmetic  19.9 us (5%)
  between operations  13.5 us (3%)
    all_to_all x1, blocking collectives, per_device(): lax.all_to_all(outgoing, 'slab', split_axis=1, concat_axis=1, tiled=True)  121 us
    dot_general x1, matrix products, per_device(): lax.dot_general(ordered, v_slab, (((1,), (1,)), ((), ())), precision=lax....  105 us
    gather x2, local copies, waits for them, and re-layouts, per_device(): jnp.take(copies.reshape(row_count, -1, BLK), slot_ids, axis=1)  38.4 us
    all_gather x1, waiting for transfers between devices, per_device(): copies = lax.all_gather(arrived, 'rep', axis=1, tiled=True)  32.5 us
    reduce_scatter x1, waiting for transfers between devices, per_device(): lax.psum_scatter(partial_value, 'slab', scatter_dimension=0, tiled=True)  32.3 us
    unnamed x5, local copies, waits for them, and re-layouts  12 us
    reshape x1, local copies, waits for them, and re-layouts, per_device(): blocked = t2_stored.reshape(row_count, stored, BLK)  11.3 us
    gather x1, local copies, waits for them, and re-layouts, per_device(): picked = jnp.take(blocked, chosen.reshape(-1), axis=1)  10.9 us
  transfers between devices with their start and end apart: 2, of which 2 were waited for; matrix products, arithmetic and copies ran while one was open for 1% of the time, Pallas kernels for 0%

commit v1 on v0

v1 whole, which is shorter than its diff:
```python
import jax
import jax.numpy as jnp
from jax import lax
from jax.experimental import pallas as pl
from jax.experimental.pallas import tpu as pltpu
from jax.sharding import PartitionSpec as P

BLK = 128
CHUNK = 2
COST = 20
SPLIT = 5
PART_COST = (20, 4)
DEPTH = 4
VMEM_LIMIT = 30 * 1024 * 1024


def slot_tables(block_source, stored, blk_dev, cap, slabs, reps, slab, rep):
    nblk = block_source.shape[0]
    k = jnp.arange(nblk, dtype=jnp.int32)
    holder = block_source // stored
    owner = k // blk_dev
    key = owner * (slabs * reps) + holder
    earlier = (key[None, :] == key[:, None]) & (k[None, :] < k[:, None])
    rank = jnp.sum(earlier.astype(jnp.int32), axis=1)
    code = key * cap + rank

    me = slab * reps + rep
    slot = jnp.arange(slabs * cap, dtype=jnp.int32)
    want = (((slot // cap) ^ slab) * (slabs * reps) + me) * cap + slot % cap
    send_ids = jnp.sum(
        jnp.where(code[None, :] == want[:, None], block_source[None, :] - me * stored, 0), axis=1
    )

    slot = jnp.arange(slabs * reps * cap, dtype=jnp.int32)
    dist = slot // (reps * cap)
    other = (slot // cap) % reps
    source = (dist ^ slab) * reps + (other ^ rep)
    want = (slab * (slabs * reps) + source) * cap + slot % cap
    hit = code[None, :] == want[:, None]
    v_ids = jnp.sum(jnp.where(hit, k[None, :] - slab * blk_dev, 0), axis=1)
    filled = jnp.sum(hit.astype(jnp.int32), axis=1)
    return send_ids, v_ids, filled


def row_range(height, part):
    first = height * SPLIT // 64 * 8
    return {None: (0, height), 0: (0, first), 1: (first, height - first)}[part]


def block_copy(t2_ref, number, out, sem, part=None):
    start = pl.multiple_of(number * BLK, BLK)
    low, size = row_range(t2_ref.shape[1], part)
    copy = pltpu.make_async_copy(
        t2_ref.at[:, pl.ds(low, size), pl.ds(start, BLK)], out, sem
    )
    copy.start()
    return copy


def block_shape(t2, blocks, part=None):
    size = row_range(t2.shape[1], part)[1]
    return jax.ShapeDtypeStruct((blocks, t2.shape[0], size, BLK), t2.dtype)


def flat(x):
    return x.reshape(x.shape[0], -1, BLK)


def pack_blocks(t2, send_ids, groups):
    total = sum(len(g) for g in groups)

    def body(ids, src, *rest):
        outs, sems = rest[:-1], rest[-1]
        copies = []
        for out, group in zip(outs, groups):
            for j, slot in enumerate(group):
                copies.append(block_copy(src, ids[slot], out.at[j], sems.at[len(copies)]))
        for copy in copies:
            copy.wait()

    packed = pl.pallas_call(
        body,
        out_shape=[block_shape(t2, len(g)) for g in groups],
        in_specs=[
            pl.BlockSpec(memory_space=pltpu.SMEM),
            pl.BlockSpec(memory_space=pltpu.HBM),
        ],
        out_specs=[pl.BlockSpec(memory_space=pltpu.VMEM)] * len(groups),
        scratch_shapes=[pltpu.SemaphoreType.DMA((total,))],
        compiler_params=pltpu.CompilerParams(vmem_limit_bytes=VMEM_LIMIT),
        cost_estimate=pl.CostEstimate(
            flops=0, bytes_accessed=2 * total * t2.shape[0] * t2.shape[1] * BLK * 4, transcendentals=0
        ),
        name="pack",
    )(send_ids, t2)
    return [flat(x) for x in packed]


def split(x):
    high = x.astype(jnp.bfloat16)
    return high, (x - high.astype(jnp.float32)).astype(jnp.bfloat16)


def dot(a, b):
    dims = (((1,), (1,)), ((), ()))
    return lax.dot_general(a, b, dims, preferred_element_type=jnp.float32)


def prepare(v, tables, slot_groups):
    _, v_ids, _ = tables
    cols = v.shape[0]
    total = sum(len(g) for g in slot_groups)

    def body(ids, v_ref, *refs):
        outs, (v_buf, sems) = refs[:-2], refs[-2:]
        copies = []
        for group in slot_groups:
            for slot in group:
                start = pl.multiple_of(ids[slot] * BLK, BLK)
                at = len(copies)
                copies.append(
                    pltpu.make_async_copy(
                        v_ref.at[:, pl.ds(start, BLK)], v_buf.at[at], sems.at[at]
                    )
                )
                copies[-1].start()
        n = 0
        for group, out in zip(slot_groups, outs):
            for j in range(len(group)):
                copies[n].wait()
                high, low = split(v_buf[n])
                out[:, pl.ds(j * BLK, BLK)] = high
                out[:, pl.ds((len(group) + j) * BLK, BLK)] = low
                n += 1

    return pl.pallas_call(
        body,
        out_shape=[
            jax.ShapeDtypeStruct((cols, 2 * len(g) * BLK), jnp.bfloat16) for g in slot_groups
        ],
        in_specs=[
            pl.BlockSpec(memory_space=pltpu.SMEM),
            pl.BlockSpec(memory_space=pltpu.HBM),
        ],
        out_specs=[pl.BlockSpec(memory_space=pltpu.VMEM)] * len(slot_groups),
        scratch_shapes=[
            pltpu.VMEM((total, cols, BLK), jnp.float32),
            pltpu.SemaphoreType.DMA((total,)),
        ],
        compiler_params=pltpu.CompilerParams(vmem_limit_bytes=VMEM_LIMIT),
        cost_estimate=pl.CostEstimate(
            flops=0, bytes_accessed=8 * total * cols * BLK, transcendentals=0
        ),
        name="prepare",
    )(v_ids, v)


def add_products(
    acc,
    parts,
    t2,
    v,
    tables,
    position,
    ready=None,
    turn=False,
    part=None,
    base=None,
    pass_on=0,
    fetch=(),
    cost=1,
):
    send_ids, v_ids, filled = tables
    where = [(i, n, slot) for i, (_, slots) in enumerate(parts) for n, slot in enumerate(slots)]
    slabs, height = t2.shape[:2]
    low, size = row_range(height, part)
    rows = slabs * size
    cols = v.shape[0]
    count = len(where)
    arrays = [x for x, _ in parts if x is not None]
    passed = sum(len(slots) for _, slots in parts[:pass_on])
    own = [n for n, (i, _, _) in enumerate(where) if parts[i][0] is None]
    fetched = len(own) + sum(len(g) for g, _ in fetch)
    results = 1 if base is None else slabs
    turned_here = turn or base is not None

    def body(*refs):
        refs = list(refs)
        ids, mask, sends, place, v_ref, t2_ref = refs[:6]
        del refs[:6]
        acc_ref = refs.pop(0) if acc is not None else None
        base_ref = refs.pop(0) if base is not None else None
        ready_ref = refs.pop(0) if ready is not None else None
        t_refs = [None if x is None else refs.pop(0) for x, _ in parts]
        v_buf, total, turned, v_sems, t_sems = refs[-5:]
        outs = refs[:-5]
        pass_ref = outs[results] if pass_on else None
        fetch_refs = outs[results + (pass_on > 0) :]

        v_copies, own_copies, late_copies = [], {}, []
        for n, (i, at, slot) in enumerate(where):
            if n in own:
                sem = t_sems.at[len(own_copies)]
                own_copies[n] = block_copy(t2_ref, sends[at], pass_ref.at[n], sem)
            if ready is not None:
                continue
            start = pl.multiple_of(ids[slot] * BLK, BLK)
            copy = pltpu.make_async_copy(v_ref.at[:, pl.ds(start, BLK)], v_buf.at[n], v_sems.at[n])
            copy.start()
            v_copies.append(copy)
        for (group, piece), out in zip(fetch, fetch_refs):
            for j, slot in enumerate(group):
                sem = t_sems.at[len(own) + len(late_copies)]
                late_copies.append(block_copy(t2_ref, sends[slot], out.at[j], sem, piece))

        def amplitudes(n):
            i, at, slot = where[n]
            if n in own:
                own_copies[n].wait()
                x = pass_ref[n].reshape(rows, BLK)
            else:
                x = t_refs[i][at]
            if filled is not None:
                x = jnp.where(mask[slot] > 0, x, 0.0)
            return x

        out_ref = total if turned_here else outs[0]
        depth = DEPTH if ready is None else count
        for n in range(0, count, depth):
            group = range(n, min(n + depth, count))
            t_high, t_low = split(jnp.concatenate([amplitudes(m) for m in group], axis=1))
            if ready is None:
                for m in group:
                    v_copies[m].wait()
                v_high, v_low = split(jnp.concatenate([v_buf[m] for m in group], axis=1))
                both = jnp.concatenate([v_high, v_low], axis=1)
            else:
                both, v_high = ready_ref[...], ready_ref[:, pl.ds(0, count * BLK)]
            product = dot(both, jnp.concatenate([t_high, t_high], axis=1)) + dot(v_high, t_low)
            if n > 0:
                out_ref[...] += product
            elif acc is None:
                out_ref[...] = product
            else:
                out_ref[...] = acc_ref[...] + product
        if turn:
            outs[0][...] = jnp.transpose(total[...])
        if base is not None:
            turned[...] = jnp.transpose(total[...])
            for d in range(slabs):
                owner = place[0] ^ d
                here = pl.multiple_of(owner * size, 8)
                there = pl.multiple_of(owner * height + low, 8)
                outs[d][...] = base_ref[pl.ds(there, size), :] + turned[pl.ds(here, size), :]
        for copy in late_copies:
            copy.wait()

    shapes = [(rows, cols) if turn else (cols, rows)] if base is None else [(size, cols)] * slabs
    out_shape = [jax.ShapeDtypeStruct(shape, jnp.float32) for shape in shapes]
    if pass_on:
        out_shape.append(block_shape(t2, passed))
    out_shape += [block_shape(t2, len(g), piece) for g, piece in fetch]
    whole = pl.BlockSpec(memory_space=pltpu.VMEM)
    operands = [v_ids, v_ids if filled is None else filled, send_ids, position, v, t2]
    specs = [pl.BlockSpec(memory_space=pltpu.SMEM)] * 4 + [pl.BlockSpec(memory_space=pltpu.HBM)] * 2
    if acc is not None:
        operands.append(acc)
        specs.append(whole)
    if base is not None:
        operands.append(base)
        specs.append(whole)
    if ready is not None:
        operands.append(ready)
        specs.append(whole)
    operands += arrays
    specs += [whole] * len(arrays)
    result = pl.pallas_call(
        body,
        out_shape=out_shape,
        in_specs=specs,
        out_specs=[whole] * len(out_shape),
        scratch_shapes=[
            pltpu.VMEM((count, cols, BLK) if ready is None else (1, 8, BLK), jnp.float32),
            pltpu.VMEM((cols, rows) if turned_here else (8, BLK), jnp.float32),
            pltpu.VMEM((8, BLK) if base is None else (rows, cols), jnp.float32),
            pltpu.SemaphoreType.DMA((count,)),
            pltpu.SemaphoreType.DMA((max(fetched, 1),)),
        ],
        compiler_params=pltpu.CompilerParams(vmem_limit_bytes=VMEM_LIMIT),
        cost_estimate=pl.CostEstimate(
            flops=6 * count * rows * cols * BLK * cost,
            bytes_accessed=4 * (count * BLK * (rows + cols) + 2 * rows * cols) * cost,
            transcendentals=0,
        ),
        name="products",
    )(*operands)
    return [*result[:results], *(flat(x) for x in result[results:])]


def cut(cap):
    size = min(CHUNK, cap // 2)
    edges = [*range(0, cap, size), cap]
    return list(zip(edges[:-1], edges[1:]))


def per_device(t2_stored, v_slab, block_source, r_in):
    slabs = lax.axis_size("slab")
    reps = lax.axis_size("rep")
    slab = lax.axis_index("slab")
    rep = lax.axis_index("rep")
    stored = t2_stored.shape[1] // BLK
    t2_stored = t2_stored.reshape(slabs, -1, t2_stored.shape[1])
    t2_stored = pltpu.with_memory_space_constraint(t2_stored, pltpu.HBM)
    blk_dev = v_slab.shape[1] // BLK
    cap = max(2, stored // slabs)
    send_ids, v_ids, filled = slot_tables(
        block_source, stored, blk_dev, cap, slabs, reps, slab, rep
    )
    v_ids = v_ids.reshape(slabs, reps, cap)
    filled = filled.reshape(slabs, reps, cap)
    if slabs * cap == stored:
        filled = None
    tables = (send_ids, v_ids, filled)
    position = jnp.stack([slab, rep]).astype(jnp.int32)

    def over_slab(x, d):
        return lax.ppermute(x, "slab", [(i, i ^ d) for i in range(slabs)])

    def over_rep(x, slots):
        return [
            (
                lax.ppermute(x, "rep", [(i, i ^ e) for i in range(reps)]),
                [(d, e, j) for d, _, j in slots],
            )
            for e in range(1, reps)
        ]

    def products(acc, parts, **kwargs):
        return add_products(acc, parts, t2_stored, v_slab, tables, position, **kwargs)

    spans = cut(cap)
    dists = range(slabs - 1, 0, -1)
    n = len(dists)
    end = len(spans) - 1

    def slots(c):
        return [[(d, 0, j) for j in range(*spans[c])] for d in dists]

    def places(c):
        groups = [[d * cap + j for d, _, j in g] for g in slots(c)] if c <= end else []
        return [(g, p) for p in ([0, 1] if c == end else [None]) for g in groups]

    def send(packed):
        return [over_slab(x, d) for x, d in zip(packed, [*dists] * 2)]

    def at_once(arrived, groups):
        return over_rep(jnp.concatenate(arrived, axis=0), [s for g in groups for s in g])

    packed = pack_blocks(t2_stored, send_ids, [g for g, _ in places(0)])
    landed = [send(packed)]
    packed, tables = lax.optimization_barrier((packed, tables))
    own_slots = [(0, 0, j) for j in range(cap)]
    acc, passed, *packed = products(None, [(None, own_slots)], pass_on=1, fetch=places(1), cost=COST)
    older = over_rep(passed, own_slots)
    ready = {}

    def prepare_ahead(c, acc):
        own = [s for g in slots(c) for s in g]
        others = [(d, e, j) for e in range(1, reps) for d, _, j in own]
        ids, acc = lax.optimization_barrier((v_ids, acc))
        blocks = prepare(v_slab, (send_ids, ids, filled), [own, others])
        ready[c], acc = lax.optimization_barrier((blocks, acc))
        return acc

    for c in range(end):
        if c + 1 == end:
            landed.append(send(packed[:n]))
            late = packed[n:]
        else:
            landed.append(send(packed))
        arrived, acc = lax.optimization_barrier((landed[c], acc))
        siblings = at_once(arrived, slots(c))
        acc, *packed = products(
            acc,
            list(zip(arrived, slots(c))),
            fetch=places(c + 2),
            ready=ready.get(c, (None,))[0],
            cost=COST,
        )
        if c + 1 == end:
            late, acc = lax.optimization_barrier((late, acc))
            landed.append(send(late))
        if c == 0:
            (acc,) = products(acc, older, cost=0)
        kwargs = {"ready": ready.get(c, (None, None))[1], "turn": c + 1 == end}
        (acc,) = products(acc, siblings, cost=0, **kwargs)
        if c == max(end - 3, 0) and end > 1:
            acc = prepare_ahead(end - 1, acc)
        if c == max(end - 2, 0):
            acc = prepare_ahead(end, acc)
    result = []
    for part in (0, 1):
        arrived, acc = lax.optimization_barrier((landed[end + part], acc))
        others = at_once(arrived, slots(end))
        first, second = ready[end]
        (sums,) = products(
            None, list(zip(arrived, slots(end))), ready=first, part=part, cost=PART_COST[part]
        )
        sums = products(
            sums, others, ready=second, base=acc, part=part, cost=COST * (1 - part)
        )
        sums, acc = lax.optimization_barrier((sums, acc))
        low, size = row_range(r_in.shape[0], part)
        own = r_in[low : low + size] + sums[0]
        for d in dists:
            own = own + over_slab(sums[d], d)
        result.append(own)
    return jnp.concatenate(result, axis=0)


def solution(mesh):
    in_specs = (P("row", ("slab", "rep")), P("rep", "slab"), P(), P(("row", "slab"), "rep"))
    out_specs = P(("row", "slab"), "rep")
    return jax.shard_map(
        per_device, mesh=mesh, in_specs=in_specs, out_specs=out_specs, check_vma=False
    )
```

time: 402 us -> 143 us (0.36)
  blocking collectives: 121 us -> 0 us
  matrix products: 105 us -> 0 us
  local copies, waits for them, and re-layouts: 77.2 us -> 0.09 us
  Pallas kernels: 0 us -> 63.9 us
  starting transfers between devices: 0.04 us -> 36.8 us
  waiting for transfers between devices: 64.9 us -> 38.8 us
  other arithmetic: 19.9 us -> 2.81 us
  between operations: 13.5 us -> 0.34 us
    all_to_all x1 -> x0, blocking collectives: 121 us -> none  [per_device(): lax.all_to_all(outgoing, 'slab', split_axis=1, concat_axis=1, tiled=True)]
    dot_general x1 -> x0, matrix products: 105 us -> none  [per_device(): lax.dot_general(ordered, v_slab, (((1,), (1,)), ((), ())), precision=lax....]
    pallas_call x0 -> x17, Pallas kernels: none -> 63.9 us  [the longest x14 55.6 us: add_products(): pl.pallas_call(body, out_shape=out_shape, in_specs=specs, out_specs=[whol...]
    gather x7 -> x0, local copies, waits for them, and re-layouts: 53.4 us -> none  [the longest x2 38.4 us: per_device(): jnp.take(copies.reshape(row_count, -1, BLK), slot_ids, axis=1)]
    ppermute x0 -> x31, waiting for transfers between devices: none -> 38.8 us  [the longest x24 38.8 us: over_slab(): return lax.ppermute(x, 'slab', [(i, i ^ d) for i in range(slabs)])]
    ppermute x0 -> x31, starting transfers between devices: none -> 36.8 us  [the longest x24 35.9 us: over_slab(): return lax.ppermute(x, 'slab', [(i, i ^ d) for i in range(slabs)])]
    all_gather x1 -> x0, waiting for transfers between devices: 32.5 us -> none  [per_device(): copies = lax.all_gather(arrived, 'rep', axis=1, tiled=True)]
    reduce_scatter x1 -> x0, waiting for transfers between devices: 32.3 us -> none  [per_device(): lax.psum_scatter(partial_value, 'slab', scatter_dimension=0, tiled=True)]
  transfers between devices with their start and end apart: 2 -> 31, of which waited for: 2 -> 14; matrix products, arithmetic and copies ran while one was open for 1% -> 1% of each run, Pallas kernels for 0% -> 43%
where the time goes in v1:
time: 143 us
  Pallas kernels  63.9 us (45%)
  waiting for transfers between devices  38.8 us (27%)
  starting transfers between devices  36.8 us (26%)
  other arithmetic  2.81 us (2%)
    pallas_call x14, Pallas kernels, add_products(): pl.pallas_call(body, out_shape=out_shape, in_specs=specs, out_specs=[whol...  55.6 us
    ppermute x24, waiting for transfers between devices, over_slab(): return lax.ppermute(x, 'slab', [(i, i ^ d) for i in range(slabs)])  38.8 us
    ppermute x24, starting transfers between devices, over_slab(): return lax.ppermute(x, 'slab', [(i, i ^ d) for i in range(slabs)])  35.9 us
    pallas_call x2, Pallas kernels, prepare(): pl.pallas_call(body, out_shape=[jax.ShapeDtypeStruct((cols, 2 * len(g) *...  6.32 us
  transfers between devices with their start and end apart: 31, of which 14 were waited for; matrix products, arithmetic and copies ran while one was open for 1% of the time, Pallas kernels for 43%

profile of v1, /device:TPU:0, one launch (start us, length us, event | category | flops | bytes accessed | tf_op | source)
XLA Modules:
  0.0 142.8 jit_solution(10164503396268529411)
XLA Ops:
  0.0 0.7 fusion.2
  1.1 2.0 %pack.1 = (f32[2,4,128,128]{3,2,1,0:T(8,128)S(1)}, f32[2,4,128,128]{3,2,1,0:T(8,128)S(1)}, f32[2,4,128,128]{3,2,1,0:T(8,128)S(1)}) custom-call(s32[40]{0:T(128)S(1)} %select_reduce_fusion.1.ids.refs_2_, f32[4,128,5120]{2,1,0:T(8,128)} %bitcast.41), custom_call_target="tpu_custom_call" | custom-call | bytes 3145728 | tf_op jit(solution)/shard_map/pack/pallas_call | solution.py:81
  3.1 3.0 %collective-permute-start.1 = (f32[2,512,128]{2,1,0:T(8,128)S(1)}, f32[2,512,128]{2,1,0:T(8,128)S(1)}, u32[]{:S(2)}, u32[]{:S(2)}) collective-permute-start(f32[2,512,128]{2,1,0:T(8,128)S(1)} %bitcast.34), channel_id=1, source_target_pairs={{0,4},{2,6},{4,0},{6,2},{1,5},{3,7},{5,1},{7,3},{8,12},{10,14},{12... | collective-permute-start | bytes 1572872 | tf_op jit(solution)/shard_map/ppermute | solution.py:327
  6.1 1.4 %collective-permute-start = (f32[2,512,128]{2,1,0:T(8,128)S(1)}, f32[2,512,128]{2,1,0:T(8,128)S(1)}, u32[]{:S(2)}, u32[]{:S(2)}) collective-permute-start(f32[2,512,128]{2,1,0:T(8,128)S(1)} %bitcast.33), channel_id=1, source_target_pairs={{0,6},{2,4},{4,2},{6,0},{1,7},{3,5},{5,3},{7,1},{8,14},{10,12},{12... | collective-permute-start | bytes 1572872 | tf_op jit(solution)/shard_map/ppermute | solution.py:327
  8.1 6.8 %products.14 = (f32[768,512]{1,0:T(8,128)S(1)}, f32[10,4,128,128]{3,2,1,0:T(8,128)S(1)}, f32[2,4,128,128]{3,2,1,0:T(8,128)S(1)}, f32[2,4,128,128]{3,2,1,0:T(8,128)S(1)}, f32[2,4,128,128]{3,2,1,0:T(8,128)S(1)}) custom-call(s32[4,2,10]{2,1,0:T(2,128)S(1)} %reshape.142.refs_0_.refs_1_.ids, s32[4,2,10]{2,1,0:T(2,128)S(1)} %reshape.142.refs_0_.refs_1_.ids, ...), custom_call_target="tpu_custom_call" | custom-call | flops 60397977600 | bytes 193986560 | tf_op jit(solution)/shard_map/products/pallas_call | solution.py:277
  14.8 2.9 %collective-permute-start.6 = (f32[2,512,128]{2,1,0:T(8,128)S(1)}, f32[2,512,128]{2,1,0:T(8,128)S(1)}, u32[]{:S(2)}, u32[]{:S(2)}) collective-permute-start(f32[2,512,128]{2,1,0:T(8,128)S(1)} %bitcast.31), channel_id=1, source_target_pairs={{0,6},{2,4},{4,2},{6,0},{1,7},{3,5},{5,3},{7,1},{8,14},{10,12},{12... | collective-permute-start | bytes 1572872 | tf_op jit(solution)/shard_map/ppermute | solution.py:327
  18.3 12.1 %collective-permute-done.1.refs_8_ = f32[2,512,128]{2,1,0:T(8,128)S(1)} collective-permute-done((f32[2,512,128]{2,1,0:T(8,128)S(1)}, f32[2,512,128]{2,1,0:T(8,128)S(1)}, u32[]{:S(2)}, u32[]{:S(2)}) %collective-permute-start.1) | collective-permute-done | bytes 524320 | tf_op jit(solution)/shard_map/ppermute | solution.py:327
  30.3 2.2 %collective-permute-start.8 = (f32[2,512,128]{2,1,0:T(8,128)S(1)}, f32[2,512,128]{2,1,0:T(8,128)S(1)}, u32[]{:S(2)}, u32[]{:S(2)}) collective-permute-start(f32[2,512,128]{2,1,0:T(8,128)S(1)} %bitcast.27), channel_id=1, source_target_pairs={{0,2},{2,0},{4,6},{6,4},{1,3},{3,1},{5,7},{7,5},{8,10},{10,8},{12,... | collective-permute-start | bytes 1572872 | tf_op jit(solution)/shard_map/ppermute | solution.py:327
  32.7 0.6 collective-permute-start.10
  33.2 4.7 %products.15 = (f32[768,512]{1,0:T(8,128)S(1)}, f32[2,4,128,128]{3,2,1,0:T(8,128)S(1)}, f32[2,4,128,128]{3,2,1,0:T(8,128)S(1)}, f32[2,4,128,128]{3,2,1,0:T(8,128)S(1)}) custom-call(s32[4,2,10]{2,1,0:T(2,128)S(1)} %reshape.142.refs_0_.refs_1_.ids, s32[4,2,10]{2,1,0:T(2,128)S(1)} %reshape.142.refs_0_.refs_1_.ids, s32[40]{0:T(128)S(1)} %select_reduce_fusion.1.ids.refs_2_, ...), custom_call_target="tpu_custom_call" | custom-call | flops 36238786560 | bytes 141557760 | tf_op jit(solution)/shard_map/products/pallas_call | solution.py:277
  37.9 2.6 %collective-permute-start.4 = (f32[2,512,128]{2,1,0:T(8,128)S(1)}, f32[2,512,128]{2,1,0:T(8,128)S(1)}, u32[]{:S(2)}, u32[]{:S(2)}) collective-permute-start(f32[2,512,128]{2,1,0:T(8,128)S(1)} %bitcast.28), channel_id=1, source_target_pairs={{0,4},{2,6},{4,0},{6,2},{1,5},{3,7},{5,1},{7,3},{8,12},{10,14},{12... | collective-permute-start | bytes 1572872 | tf_op jit(solution)/shard_map/ppermute | solution.py:327
  40.6 5.9 %products.16.refs_6_ = f32[768,512]{1,0:T(8,128)S(1)} custom-call(s32[4,2,10]{2,1,0:T(2,128)S(1)} %reshape.142.refs_0_.refs_1_.ids, s32[4,2,10]{2,1,0:T(2,128)S(1)} %reshape.142.refs_0_.refs_1_.ids, s32[40]{0:T(128)S(1)} %select_reduce_fusion.1.ids.refs_2_, s32[2]{0:T(128)S(1)} %pad_add_fusion.refs_3_, f32[768,10240]{1,0:T(8,128)} %refs_4_.27, ...), custom_call_target="tpu_custom_call" | custom-call | tf_op jit(solution)/shard_map/products/pallas_call | solution.py:277
  46.6 4.4 %products.17.refs_6_ = f32[768,512]{1,0:T(8,128)S(1)} custom-call(s32[4,2,10]{2,1,0:T(2,128)S(1)} %reshape.142.refs_0_.refs_1_.ids, s32[4,2,10]{2,1,0:T(2,128)S(1)} %reshape.142.refs_0_.refs_1_.ids, s32[40]{0:T(128)S(1)} %select_reduce_fusion.1.ids.refs_2_, s32[2]{0:T(128)S(1)} %pad_add_fusion.refs_3_, f32[768,10240]{1,0:T(8,128)} %refs_4_.27, ...), custom_call_target="tpu_custom_call" | custom-call | tf_op jit(solution)/shard_map/products/pallas_call | solution.py:277
  51.0 1.5 %collective-permute-start.5 = (f32[2,512,128]{2,1,0:T(8,128)S(1)}, f32[2,512,128]{2,1,0:T(8,128)S(1)}, u32[]{:S(2)}, u32[]{:S(2)}) collective-permute-start(f32[2,512,128]{2,1,0:T(8,128)S(1)} %bitcast.23), channel_id=1, source_target_pairs={{0,2},{2,0},{4,6},{6,4},{1,3},{3,1},{5,7},{7,5},{8,10},{10,8},{12,... | collective-permute-start | bytes 1572872 | tf_op jit(solution)/shard_map/ppermute | solution.py:327
  52.8 1.5 %collective-permute-done.8.refs_9_ = f32[2,512,128]{2,1,0:T(8,128)S(1)} collective-permute-done((f32[2,512,128]{2,1,0:T(8,128)S(1)}, f32[2,512,128]{2,1,0:T(8,128)S(1)}, u32[]{:S(2)}, u32[]{:S(2)}) %collective-permute-start.8) | collective-permute-done | bytes 524320 | tf_op jit(solution)/shard_map/ppermute | solution.py:327
  54.4 4.9 %products.18 = (f32[768,512]{1,0:T(8,128)S(1)}, f32[2,4,128,128]{3,2,1,0:T(8,128)S(1)}, f32[2,4,128,128]{3,2,1,0:T(8,128)S(1)}, f32[2,4,128,128]{3,2,1,0:T(8,128)S(1)}) custom-call(s32[4,2,10]{2,1,0:T(2,128)S(1)} %reshape.142.refs_0_.refs_1_.ids, s32[4,2,10]{2,1,0:T(2,128)S(1)} %reshape.142.refs_0_.refs_1_.ids, s32[40]{0:T(128)S(1)} %select_reduce_fusion.1.ids.refs_2_, ...), custom_call_target="tpu_custom_call" | custom-call | flops 36238786560 | bytes 141557760 | tf_op jit(solution)/shard_map/products/pallas_call | solution.py:277
  59.3 3.0 %collective-permute-start.16 = (f32[2,512,128]{2,1,0:T(8,128)S(1)}, f32[2,512,128]{2,1,0:T(8,128)S(1)}, u32[]{:S(2)}, u32[]{:S(2)}) collective-permute-start(f32[2,512,128]{2,1,0:T(8,128)S(1)} %bitcast.29), channel_id=1, source_target_pairs={{0,6},{2,4},{4,2},{6,0},{1,7},{3,5},{5,3},{7,1},{8,14},{10,12},{12... | collective-permute-start | bytes 1572872 | tf_op jit(solution)/shard_map/ppermute | solution.py:327
  62.8 4.4 %products.19.refs_6_ = f32[768,512]{1,0:T(8,128)S(1)} custom-call(s32[4,2,10]{2,1,0:T(2,128)S(1)} %reshape.142.refs_0_.refs_1_.ids, s32[4,2,10]{2,1,0:T(2,128)S(1)} %reshape.142.refs_0_.refs_1_.ids, s32[40]{0:T(128)S(1)} %select_reduce_fusion.1.ids.refs_2_, s32[2]{0:T(128)S(1)} %pad_add_fusion.refs_3_, f32[768,10240]{1,0:T(8,128)} %refs_4_.27, ...), custom_call_target="tpu_custom_call" | custom-call | tf_op jit(solution)/shard_map/products/pallas_call | solution.py:277
  67.2 3.2 %prepare.2 = (bf16[768,1536]{1,0:T(8,128)(2,1)S(1)}, bf16[768,1536]{1,0:T(8,128)(2,1)S(1)}) custom-call(s32[4,2,10]{2,1,0:T(2,128)S(1)} %reshape.142.refs_0_.refs_1_.ids, f32[768,10240]{1,0:T(8,128)} %refs_4_.27), custom_call_target="tpu_custom_call" | custom-call | bytes 9437184 | tf_op jit(solution)/shard_map/prepare/pallas_call | solution.py:136
  70.3 4.9 %collective-permute-done.4.refs_8_ = f32[2,512,128]{2,1,0:T(8,128)S(1)} collective-permute-done((f32[2,512,128]{2,1,0:T(8,128)S(1)}, f32[2,512,128]{2,1,0:T(8,128)S(1)}, u32[]{:S(2)}, u32[]{:S(2)}) %collective-permute-start.4) | collective-permute-done | bytes 524320 | tf_op jit(solution)/shard_map/ppermute | solution.py:327
  75.2 2.2 %collective-permute-start.18 = (f32[2,512,128]{2,1,0:T(8,128)S(1)}, f32[2,512,128]{2,1,0:T(8,128)S(1)}, u32[]{:S(2)}, u32[]{:S(2)}) collective-permute-start(f32[2,512,128]{2,1,0:T(8,128)S(1)} %bitcast.24), channel_id=1, source_target_pairs={{0,2},{2,0},{4,6},{6,4},{1,3},{3,1},{5,7},{7,5},{8,10},{10,8},{12,... | collective-permute-start | bytes 1572872 | tf_op jit(solution)/shard_map/ppermute | solution.py:327
  77.6 4.5 %products.20 = (f32[768,512]{1,0:T(8,128)S(1)}, f32[2,4,80,128]{3,2,1,0:T(8,128)S(1)}, f32[2,4,80,128]{3,2,1,0:T(8,128)S(1)}, f32[2,4,80,128]{3,2,1,0:T(8,128)S(...) custom-call(s32[4,2,10]{2,1,0:T(2,128)S(1)} %reshape.142.refs_0_.refs_1_.ids, ...), custom_call_target="tpu_custom_call" | custom-call | flops 36238786560 | bytes 141557760 | tf_op jit(solution)/shard_map/products/pallas_call | solution.py:277
  82.1 2.3 %collective-permute-start.13 = (f32[2,320,128]{2,1,0:T(8,128)S(1)}, f32[2,320,128]{2,1,0:T(8,128)S(1)}, u32[]{:S(2)}, u32[]{:S(2)}) collective-permute-start(f32[2,320,128]{2,1,0:T(8,128)S(1)} %bitcast.37), channel_id=1, source_target_pairs={{0,6},{2,4},{4,2},{6,0},{1,7},{3,5},{5,3},{7,1},{8,14},{10,12},{12... | collective-permute-start | bytes 983048 | tf_op jit(solution)/shard_map/ppermute | solution.py:327
  84.9 4.4 %products.21.refs_6_ = f32[768,512]{1,0:T(8,128)S(1)} custom-call(s32[4,2,10]{2,1,0:T(2,128)S(1)} %reshape.142.refs_0_.refs_1_.ids, s32[4,2,10]{2,1,0:T(2,128)S(1)} %reshape.142.refs_0_.refs_1_.ids, s32[40]{0:T(128)S(1)} %select_reduce_fusion.1.ids.refs_2_, s32[2]{0:T(128)S(1)} %pad_add_fusion.refs_3_, f32[768,10240]{1,0:T(8,128)} %refs_4_.27, ...), custom_call_target="tpu_custom_call" | custom-call | tf_op jit(solution)/shard_map/products/pallas_call | solution.py:277
  89.3 3.2 %prepare.3 = (bf16[768,1536]{1,0:T(8,128)(2,1)S(1)}, bf16[768,1536]{1,0:T(8,128)(2,1)S(1)}) custom-call(s32[4,2,10]{2,1,0:T(2,128)S(1)} %reshape.142.refs_0_.refs_1_.ids, f32[768,10240]{1,0:T(8,128)} %refs_4_.27), custom_call_target="tpu_custom_call" | custom-call | bytes 9437184 | tf_op jit(solution)/shard_map/prepare/pallas_call | solution.py:136
  92.5 1.3 collective-permute-start.15
  93.8 3.8 %collective-permute-done.17.refs_9_ = f32[2,512,128]{2,1,0:T(8,128)S(1)} collective-permute-done((f32[2,512,128]{2,1,0:T(8,128)S(1)}, f32[2,512,128]{2,1,0:T(8,128)S(1)}, u32[]{:S(2)}, u32[]{:S(2)}) %collective-permute-start.17) | collective-permute-done | bytes 524320 | tf_op jit(solution)/shard_map/ppermute | solution.py:327
  97.6 1.6 %collective-permute-done.18.refs_10_ = f32[2,512,128]{2,1,0:T(8,128)S(1)} collective-permute-done((f32[2,512,128]{2,1,0:T(8,128)S(1)}, f32[2,512,128]{2,1,0:T(8,128)S(1)}, u32[]{:S(2)}, u32[]{:S(2)}) %collective-permute-start.18) | collective-permute-done | bytes 524320 | tf_op jit(solution)/shard_map/ppermute | solution.py:327
  99.4 2.8 %products.22.refs_6_ = f32[768,512]{1,0:T(8,128)S(1)} custom-call(s32[4,2,10]{2,1,0:T(2,128)S(1)} %reshape.142.refs_0_.refs_1_.ids, s32[4,2,10]{2,1,0:T(2,128)S(1)} %reshape.142.refs_0_.refs_1_.ids, s32[40]{0:T(128)S(1)} %select_reduce_fusion.1.ids.refs_2_, s32[2]{0:T(128)S(1)} %pad_add_fusion.refs_3_, f32[768,10240]{1,0:T(8,128)} %refs_4_.27, ...), custom_call_target="tpu_custom_call" | custom-call | flops 36238786560 | bytes 141557760 | tf_op jit(solution)/shard_map/products/pallas_call | solution.py:277
  102.2 3.0 %collective-permute-start.24 = (f32[2,192,128]{2,1,0:T(8,128)S(1)}, f32[2,192,128]{2,1,0:T(8,128)S(1)}, u32[]{:S(2)}, u32[]{:S(2)}) collective-permute-start(f32[2,192,128]{2,1,0:T(8,128)S(1)} %bitcast.40), channel_id=1, source_target_pairs={{0,6},{2,4},{4,2},{6,0},{1,7},{3,5},{5,3},{7,1},{8,14},{10,12},{12... | collective-permute-start | bytes 589832 | tf_op jit(solution)/shard_map/ppermute | solution.py:327
  105.7 3.1 %products.23.refs_7_ = f32[512,768]{1,0:T(8,128)S(1)} custom-call(s32[4,2,10]{2,1,0:T(2,128)S(1)} %reshape.142.refs_0_.refs_1_.ids, s32[4,2,10]{2,1,0:T(2,128)S(1)} %reshape.142.refs_0_.refs_1_.ids, s32[40]{0:T(128)S(1)} %select_reduce_fusion.1.ids.refs_2_, s32[2]{0:T(128)S(1)} %pad_add_fusion.refs_3_, f32[768,10240]{1,0:T(8,128)} %refs_4_.27, ...), custom_call_target="tpu_custom_call" | custom-call | tf_op jit(solution)/shard_map/products/pallas_call | solution.py:277
  108.8 0.7 collective-permute-start.26
  109.4 2.2 %collective-permute-done.14.refs_8_ = f32[2,320,128]{2,1,0:T(8,128)S(1)} collective-permute-done((f32[2,320,128]{2,1,0:T(8,128)S(1)}, f32[2,320,128]{2,1,0:T(8,128)S(1)}, u32[]{:S(2)}, u32[]{:S(2)}) %collective-permute-start.14) | collective-permute-done | bytes 327712 | tf_op jit(solution)/shard_map/ppermute | solution.py:327
  111.6 1.7 %collective-permute-done.15.refs_9_ = f32[2,320,128]{2,1,0:T(8,128)S(1)} collective-permute-done((f32[2,320,128]{2,1,0:T(8,128)S(1)}, f32[2,320,128]{2,1,0:T(8,128)S(1)}, u32[]{:S(2)}, u32[]{:S(2)}) %collective-permute-start.15) | collective-permute-done | bytes 327712 | tf_op jit(solution)/shard_map/ppermute | solution.py:327
  113.5 3.0 %products.24.refs_6_ = f32[768,320]{1,0:T(8,128)S(1)} custom-call(s32[4,2,10]{2,1,0:T(2,128)S(1)} %reshape.142.refs_0_.refs_1_.ids, s32[4,2,10]{2,1,0:T(2,128)S(1)} %reshape.142.refs_0_.refs_1_.ids, s32[40]{0:T(128)S(1)} %select_reduce_fusion.1.ids.refs_2_, s32[2]{0:T(128)S(1)} %pad_add_fusion.refs_3_, f32[768,10240]{1,0:T(8,128)} %refs_4_.27, ...), custom_call_target="tpu_custom_call" | custom-call | flops 22649241600 | bytes 106168320 | tf_op jit(solution)/shard_map/products/pallas_call | solution.py:277
  116.5 3.1 %products.25 = (f32[80,768]{1,0:T(8,128)S(1)}, f32[80,768]{1,0:T(8,128)S(1)}, f32[80,768]{1,0:T(8,128)S(1)}, f32[80,768]{1,0:T(8,128)S(1)}) custom-call(s32[4,2,10]{2,1,0:T(2,128)S(1)} %reshape.142.refs_0_.refs_1_.ids, s32[4,2,10]{2,1,0:T(2,128)S(1)} %reshape.142.refs_0_.refs_1_.ids, s32[40]{0:T(128)S(1)} %select_reduce_fusion.1.ids.refs_2_, ...), custom_call_target="tpu_custom_call" | custom-call | flops 22649241600 | bytes 106168320 | tf_op jit(solution)/shard_map/products/pallas_call | solution.py:277
  119.5 1.2 collective-permute-done.26.refs_9_
  120.8 2.7 %collective-permute-start.21 = (f32[80,768]{1,0:T(8,128)S(1)}, f32[80,768]{1,0:T(8,128)S(1)}, u32[]{:S(2)}, u32[]{:S(2)}) collective-permute-start(f32[80,768]{1,0:T(8,128)S(1)} %get-tuple-element.154), channel_id=1, source_target_pairs={{0,6},{2,4},{4,2},{6,0},{1,7},{3,5},{5,3},{7,1},{8,14},{10,12},{12... | collective-permute-start | bytes 737288 | tf_op jit(solution)/shard_map/ppermute | solution.py:327
  123.5 0.5 collective-permute-start.22
  124.4 1.8 %products.26.refs_6_ = f32[768,192]{1,0:T(8,128)S(1)} custom-call(s32[4,2,10]{2,1,0:T(2,128)S(1)} %reshape.142.refs_0_.refs_1_.ids, s32[4,2,10]{2,1,0:T(2,128)S(1)} %reshape.142.refs_0_.refs_1_.ids, s32[40]{0:T(128)S(1)} %select_reduce_fusion.1.ids.refs_2_, s32[2]{0:T(128)S(1)} %pad_add_fusion.refs_3_, f32[768,10240]{1,0:T(8,128)} %refs_4_.27, ...), custom_call_target="tpu_custom_call" | custom-call | flops 2717908992 | bytes 16515072 | tf_op jit(solution)/shard_map/products/pallas_call | solution.py:277
  126.3 2.1 %products.27 = (f32[48,768]{1,0:T(8,128)S(1)}, f32[48,768]{1,0:T(8,128)S(1)}, f32[48,768]{1,0:T(8,128)S(1)}, f32[48,768]{1,0:T(8,128)S(1)}) custom-call(s32[4,2,10]{2,1,0:T(2,128)S(1)} %reshape.142.refs_0_.refs_1_.ids, s32[4,2,10]{2,1,0:T(2,128)S(1)} %reshape.142.refs_0_.refs_1_.ids, s32[40]{0:T(128)S(1)} %select_reduce_fusion.1.ids.refs_2_, ...), custom_call_target="tpu_custom_call" | custom-call | tf_op jit(solution)/shard_map/products/pallas_call | solution.py:277
  128.3 2.7 %collective-permute-start.28 = (f32[48,768]{1,0:T(8,128)S(1)}, f32[48,768]{1,0:T(8,128)S(1)}, u32[]{:S(2)}, u32[]{:S(2)}) collective-permute-start(f32[48,768]{1,0:T(8,128)S(1)} %get-tuple-element.170), channel_id=1, source_target_pairs={{0,6},{2,4},{4,2},{6,0},{1,7},{3,5},{5,3},{7,1},{8,14},{10,12},{12... | collective-permute-start | bytes 442376 | tf_op jit(solution)/shard_map/ppermute | solution.py:327
  131.0 0.5 collective-permute-start.29
  131.5 0.7 collective-permute-start.30
  132.2 3.7 %collective-permute-done.22 = f32[80,768]{1,0:T(8,128)S(1)} collective-permute-done((f32[80,768]{1,0:T(8,128)S(1)}, f32[80,768]{1,0:T(8,128)S(1)}, u32[]{:S(2)}, u32[]{:S(2)}) %collective-permute-start.22) | collective-permute-done | bytes 245792 | tf_op jit(solution)/shard_map/ppermute | solution.py:327
  136.2 2.9 %collective-permute-done.28 = f32[48,768]{1,0:T(8,128)S(1)} collective-permute-done((f32[48,768]{1,0:T(8,128)S(1)}, f32[48,768]{1,0:T(8,128)S(1)}, u32[]{:S(2)}, u32[]{:S(2)}) %collective-permute-start.28) | collective-permute-done | bytes 147488 | tf_op jit(solution)/shard_map/ppermute | solution.py:327
  139.1 2.6 %collective-permute-done.29 = f32[48,768]{1,0:T(8,128)S(1)} collective-permute-done((f32[48,768]{1,0:T(8,128)S(1)}, f32[48,768]{1,0:T(8,128)S(1)}, u32[]{:S(2)}, u32[]{:S(2)}) %collective-permute-start.29) | collective-permute-done | bytes 147488 | tf_op jit(solution)/shard_map/ppermute | solution.py:327
  142.0 0.8 pad_maximum_fusion.6
  (51 shorter events, 5.1 us)
Async XLA Ops:
  3.1 27.2 %collective-permute-start.1 = (f32[2,512,128]{2,1,0:T(8,128)S(1)}, f32[2,512,128]{2,1,0:T(8,128)S(1)}, u32[]{:S(2)}, u32[]{:S(2)}) collective-permute-start(f32[2,512,128]{2,1,0:T(8,128)S(1)} %bitcast.34), channel_id=1, source_target_pairs={{0,4},{2,6},{4,0},{6,2},{1,5},{3,7},{5,1},{7,3},{8,12},{10,14},{12... | collective-permute-start | bytes 1572872 | tf_op jit(solution)/shard_map/ppermute | solution.py:327
  6.1 26.4 %collective-permute-start = (f32[2,512,128]{2,1,0:T(8,128)S(1)}, f32[2,512,128]{2,1,0:T(8,128)S(1)}, u32[]{:S(2)}, u32[]{:S(2)}) collective-permute-start(f32[2,512,128]{2,1,0:T(8,128)S(1)} %bitcast.33), channel_id=1, source_target_pairs={{0,6},{2,4},{4,2},{6,0},{1,7},{3,5},{5,3},{7,1},{8,14},{10,12},{12... | collective-permute-start | bytes 1572872 | tf_op jit(solution)/shard_map/ppermute | solution.py:327
  7.6 25.0 %collective-permute-start.2 = (f32[2,512,128]{2,1,0:T(8,128)S(1)}, f32[2,512,128]{2,1,0:T(8,128)S(1)}, u32[]{:S(2)}, u32[]{:S(2)}) collective-permute-start(f32[2,512,128]{2,1,0:T(8,128)S(1)} %bitcast.32), channel_id=1, source_target_pairs={{0,2},{2,0},{4,6},{6,4},{1,3},{3,1},{5,7},{7,5},{8,10},{10,8},{12,... | collective-permute-start | bytes 1572872 | tf_op jit(solution)/shard_map/ppermute | solution.py:327
  14.8 36.1 %collective-permute-start.6 = (f32[2,512,128]{2,1,0:T(8,128)S(1)}, f32[2,512,128]{2,1,0:T(8,128)S(1)}, u32[]{:S(2)}, u32[]{:S(2)}) collective-permute-start(f32[2,512,128]{2,1,0:T(8,128)S(1)} %bitcast.31), channel_id=1, source_target_pairs={{0,6},{2,4},{4,2},{6,0},{1,7},{3,5},{5,3},{7,1},{8,14},{10,12},{12... | collective-permute-start | bytes 1572872 | tf_op jit(solution)/shard_map/ppermute | solution.py:327
  17.8 35.0 %collective-permute-start.7 = (f32[2,512,128]{2,1,0:T(8,128)S(1)}, f32[2,512,128]{2,1,0:T(8,128)S(1)}, u32[]{:S(2)}, u32[]{:S(2)}) collective-permute-start(f32[2,512,128]{2,1,0:T(8,128)S(1)} %bitcast.30), channel_id=1, source_target_pairs={{0,4},{2,6},{4,0},{6,2},{1,5},{3,7},{5,1},{7,3},{8,12},{10,14},{12... | collective-permute-start | bytes 1572872 | tf_op jit(solution)/shard_map/ppermute | solution.py:327
  30.3 23.9 %collective-permute-start.8 = (f32[2,512,128]{2,1,0:T(8,128)S(1)}, f32[2,512,128]{2,1,0:T(8,128)S(1)}, u32[]{:S(2)}, u32[]{:S(2)}) collective-permute-start(f32[2,512,128]{2,1,0:T(8,128)S(1)} %bitcast.27), channel_id=1, source_target_pairs={{0,2},{2,0},{4,6},{6,4},{1,3},{3,1},{5,7},{7,5},{8,10},{10,8},{12,... | collective-permute-start | bytes 1572872 | tf_op jit(solution)/shard_map/ppermute | solution.py:327
  32.6 5.4 %collective-permute-start.9 = (f32[10,512,128]{2,1,0:T(8,128)S(1)}, f32[10,512,128]{2,1,0:T(8,128)S(1)}, u32[]{:S(2)}, u32[]{:S(2)}) collective-permute-start(f32[10,512,128]{2,1,0:T(8,128)S(1)} %bitcast.22), channel_id=1, source_target_pairs={{0,1},{1,0},{2,3},{3,2},{4,5},{5,4},{6,7},{7,6},{8,9},{9,8},{10,11... | collective-permute-start | bytes 7864328 | tf_op jit(solution)/shard_map/ppermute | solution.py:332
  32.7 13.8 %collective-permute-start.10 = (f32[6,512,128]{2,1,0:T(8,128)S(1)}, f32[6,512,128]{2,1,0:T(8,128)S(1)}, u32[]{:S(2)}, u32[]{:S(2)}) collective-permute-start(f32[6,512,128]{2,1,0:T(8,128)S(1)} %pad_maximum_fusion), channel_id=1, source_target_pairs={{0,1},{1,0},{2,3},{3,2},{4,5},{5,4},{6,7},{7,6},{8,9},{9,8},{10,11... | collective-permute-start | bytes 4718600 | tf_op jit(solution)/shard_map/ppermute | solution.py:332
  37.9 37.2 %collective-permute-start.4 = (f32[2,512,128]{2,1,0:T(8,128)S(1)}, f32[2,512,128]{2,1,0:T(8,128)S(1)}, u32[]{:S(2)}, u32[]{:S(2)}) collective-permute-start(f32[2,512,128]{2,1,0:T(8,128)S(1)} %bitcast.28), channel_id=1, source_target_pairs={{0,4},{2,6},{4,0},{6,2},{1,5},{3,7},{5,1},{7,3},{8,12},{10,14},{12... | collective-permute-start | bytes 1572872 | tf_op jit(solution)/shard_map/ppermute | solution.py:327
  46.5 30.9 %collective-permute-start.3 = (f32[2,512,128]{2,1,0:T(8,128)S(1)}, f32[2,512,128]{2,1,0:T(8,128)S(1)}, u32[]{:S(2)}, u32[]{:S(2)}) collective-permute-start(f32[2,512,128]{2,1,0:T(8,128)S(1)} %bitcast.25), channel_id=1, source_target_pairs={{0,6},{2,4},{4,2},{6,0},{1,7},{3,5},{5,3},{7,1},{8,14},{10,12},{12... | collective-permute-start | bytes 1572872 | tf_op jit(solution)/shard_map/ppermute | solution.py:327
  51.0 26.4 %collective-permute-start.5 = (f32[2,512,128]{2,1,0:T(8,128)S(1)}, f32[2,512,128]{2,1,0:T(8,128)S(1)}, u32[]{:S(2)}, u32[]{:S(2)}) collective-permute-start(f32[2,512,128]{2,1,0:T(8,128)S(1)} %bitcast.23), channel_id=1, source_target_pairs={{0,2},{2,0},{4,6},{6,4},{1,3},{3,1},{5,7},{7,5},{8,10},{10,8},{12,... | collective-permute-start | bytes 1572872 | tf_op jit(solution)/shard_map/ppermute | solution.py:327
  54.3 8.0 %collective-permute-start.11 = (f32[6,512,128]{2,1,0:T(8,128)S(1)}, f32[6,512,128]{2,1,0:T(8,128)S(1)}, u32[]{:S(2)}, u32[]{:S(2)}) collective-permute-start(f32[6,512,128]{2,1,0:T(8,128)S(1)} %pad_maximum_fusion.1), channel_id=1, source_target_pairs={{0,1},{1,0},{2,3},{3,2},{4,5},{5,4},{6,7},{7,6},{8,9},{9,8},{10,11... | collective-permute-start | bytes 4718600 | tf_op jit(solution)/shard_map/ppermute | solution.py:332
  59.3 33.2 %collective-permute-start.16 = (f32[2,512,128]{2,1,0:T(8,128)S(1)}, f32[2,512,128]{2,1,0:T(8,128)S(1)}, u32[]{:S(2)}, u32[]{:S(2)}) collective-permute-start(f32[2,512,128]{2,1,0:T(8,128)S(1)} %bitcast.29), channel_id=1, source_target_pairs={{0,6},{2,4},{4,2},{6,0},{1,7},{3,5},{5,3},{7,1},{8,14},{10,12},{12... | collective-permute-start | bytes 1572872 | tf_op jit(solution)/shard_map/ppermute | solution.py:327
  62.3 35.3 %collective-permute-start.17 = (f32[2,512,128]{2,1,0:T(8,128)S(1)}, f32[2,512,128]{2,1,0:T(8,128)S(1)}, u32[]{:S(2)}, u32[]{:S(2)}) collective-permute-start(f32[2,512,128]{2,1,0:T(8,128)S(1)} %bitcast.26), channel_id=1, source_target_pairs={{0,4},{2,6},{4,0},{6,2},{1,5},{3,7},{5,1},{7,3},{8,12},{10,14},{12... | collective-permute-start | bytes 1572872 | tf_op jit(solution)/shard_map/ppermute | solution.py:327
  75.2 24.1 %collective-permute-start.18 = (f32[2,512,128]{2,1,0:T(8,128)S(1)}, f32[2,512,128]{2,1,0:T(8,128)S(1)}, u32[]{:S(2)}, u32[]{:S(2)}) collective-permute-start(f32[2,512,128]{2,1,0:T(8,128)S(1)} %bitcast.24), channel_id=1, source_target_pairs={{0,2},{2,0},{4,6},{6,4},{1,3},{3,1},{5,7},{7,5},{8,10},{10,8},{12,... | collective-permute-start | bytes 1572872 | tf_op jit(solution)/shard_map/ppermute | solution.py:327
  77.5 6.9 %collective-permute-start.12 = (f32[6,512,128]{2,1,0:T(8,128)S(1)}, f32[6,512,128]{2,1,0:T(8,128)S(1)}, u32[]{:S(2)}, u32[]{:S(2)}) collective-permute-start(f32[6,512,128]{2,1,0:T(8,128)S(1)} %pad_maximum_fusion.2), channel_id=1, source_target_pairs={{0,1},{1,0},{2,3},{3,2},{4,5},{5,4},{6,7},{7,6},{8,9},{9,8},{10,11... | collective-permute-start | bytes 4718600 | tf_op jit(solution)/shard_map/ppermute | solution.py:332
  82.1 26.7 %collective-permute-start.13 = (f32[2,320,128]{2,1,0:T(8,128)S(1)}, f32[2,320,128]{2,1,0:T(8,128)S(1)}, u32[]{:S(2)}, u32[]{:S(2)}) collective-permute-start(f32[2,320,128]{2,1,0:T(8,128)S(1)} %bitcast.37), channel_id=1, source_target_pairs={{0,6},{2,4},{4,2},{6,0},{1,7},{3,5},{5,3},{7,1},{8,14},{10,12},{12... | collective-permute-start | bytes 983048 | tf_op jit(solution)/shard_map/ppermute | solution.py:327
  84.4 27.2 %collective-permute-start.14 = (f32[2,320,128]{2,1,0:T(8,128)S(1)}, f32[2,320,128]{2,1,0:T(8,128)S(1)}, u32[]{:S(2)}, u32[]{:S(2)}) collective-permute-start(f32[2,320,128]{2,1,0:T(8,128)S(1)} %bitcast.36), channel_id=1, source_target_pairs={{0,4},{2,6},{4,0},{6,2},{1,5},{3,7},{5,1},{7,3},{8,12},{10,14},{12... | collective-permute-start | bytes 983048 | tf_op jit(solution)/shard_map/ppermute | solution.py:327
  92.5 20.8 %collective-permute-start.15 = (f32[2,320,128]{2,1,0:T(8,128)S(1)}, f32[2,320,128]{2,1,0:T(8,128)S(1)}, u32[]{:S(2)}, u32[]{:S(2)}) collective-permute-start(f32[2,320,128]{2,1,0:T(8,128)S(1)} %bitcast.35), channel_id=1, source_target_pairs={{0,2},{2,0},{4,6},{6,4},{1,3},{3,1},{5,7},{7,5},{8,10},{10,8},{12,... | collective-permute-start | bytes 983048 | tf_op jit(solution)/shard_map/ppermute | solution.py:327
  99.4 5.9 %collective-permute-start.19 = (f32[6,512,128]{2,1,0:T(8,128)S(1)}, f32[6,512,128]{2,1,0:T(8,128)S(1)}, u32[]{:S(2)}, u32[]{:S(2)}) collective-permute-start(f32[6,512,128]{2,1,0:T(8,128)S(1)} %pad_maximum_fusion.3), channel_id=1, source_target_pairs={{0,1},{1,0},{2,3},{3,2},{4,5},{5,4},{6,7},{7,6},{8,9},{9,8},{10,11... | collective-permute-start | bytes 4718600 | tf_op jit(solution)/shard_map/ppermute | solution.py:332
  102.2 17.3 %collective-permute-start.24 = (f32[2,192,128]{2,1,0:T(8,128)S(1)}, f32[2,192,128]{2,1,0:T(8,128)S(1)}, u32[]{:S(2)}, u32[]{:S(2)}) collective-permute-start(f32[2,192,128]{2,1,0:T(8,128)S(1)} %bitcast.40), channel_id=1, source_target_pairs={{0,6},{2,4},{4,2},{6,0},{1,7},{3,5},{5,3},{7,1},{8,14},{10,12},{12... | collective-permute-start | bytes 589832 | tf_op jit(solution)/shard_map/ppermute | solution.py:327
  105.2 14.3 %collective-permute-start.25 = (f32[2,192,128]{2,1,0:T(8,128)S(1)}, f32[2,192,128]{2,1,0:T(8,128)S(1)}, u32[]{:S(2)}, u32[]{:S(2)}) collective-permute-start(f32[2,192,128]{2,1,0:T(8,128)S(1)} %bitcast.39), channel_id=1, source_target_pairs={{0,4},{2,6},{4,0},{6,2},{1,5},{3,7},{5,1},{7,3},{8,12},{10,14},{12... | collective-permute-start | bytes 589832 | tf_op jit(solution)/shard_map/ppermute | solution.py:327
  108.8 11.9 %collective-permute-start.26 = (f32[2,192,128]{2,1,0:T(8,128)S(1)}, f32[2,192,128]{2,1,0:T(8,128)S(1)}, u32[]{:S(2)}, u32[]{:S(2)}) collective-permute-start(f32[2,192,128]{2,1,0:T(8,128)S(1)} %bitcast.38), channel_id=1, source_target_pairs={{0,2},{2,0},{4,6},{6,4},{1,3},{3,1},{5,7},{7,5},{8,10},{10,8},{12,... | collective-permute-start | bytes 589832 | tf_op jit(solution)/shard_map/ppermute | solution.py:327
  113.4 3.0 %collective-permute-start.20 = (f32[6,320,128]{2,1,0:T(8,128)S(1)}, f32[6,320,128]{2,1,0:T(8,128)S(1)}, u32[]{:S(2)}, u32[]{:S(2)}) collective-permute-start(f32[6,320,128]{2,1,0:T(8,128)S(1)} %pad_maximum_fusion.4), channel_id=1, source_target_pairs={{0,1},{1,0},{2,3},{3,2},{4,5},{5,4},{6,7},{7,6},{8,9},{9,8},{10,11... | collective-permute-start | bytes 2949128 | tf_op jit(solution)/shard_map/ppermute | solution.py:332
  120.7 5.5 %collective-permute-start.27 = (f32[6,192,128]{2,1,0:T(8,128)S(1)}, f32[6,192,128]{2,1,0:T(8,128)S(1)}, u32[]{:S(2)}, u32[]{:S(2)}) collective-permute-start(f32[6,192,128]{2,1,0:T(8,128)S(1)} %pad_maximum_fusion.5), channel_id=1, source_target_pairs={{0,1},{1,0},{2,3},{3,2},{4,5},{5,4},{6,7},{7,6},{8,9},{9,8},{10,11... | collective-permute-start | bytes 1769480 | tf_op jit(solution)/shard_map/ppermute | solution.py:332
  120.8 10.7 %collective-permute-start.21 = (f32[80,768]{1,0:T(8,128)S(1)}, f32[80,768]{1,0:T(8,128)S(1)}, u32[]{:S(2)}, u32[]{:S(2)}) collective-permute-start(f32[80,768]{1,0:T(8,128)S(1)} %get-tuple-element.154), channel_id=1, source_target_pairs={{0,6},{2,4},{4,2},{6,0},{1,7},{3,5},{5,3},{7,1},{8,14},{10,12},{12... | collective-permute-start | bytes 737288 | tf_op jit(solution)/shard_map/ppermute | solution.py:327
  123.5 12.4 %collective-permute-start.22 = (f32[80,768]{1,0:T(8,128)S(1)}, f32[80,768]{1,0:T(8,128)S(1)}, u32[]{:S(2)}, u32[]{:S(2)}) collective-permute-start(f32[80,768]{1,0:T(8,128)S(1)} %get-tuple-element.155), channel_id=1, source_target_pairs={{0,4},{2,6},{4,0},{6,2},{1,5},{3,7},{5,1},{7,3},{8,12},{10,14},{12... | collective-permute-start | bytes 737288 | tf_op jit(solution)/shard_map/ppermute | solution.py:327
  124.0 12.1 %collective-permute-start.23 = (f32[80,768]{1,0:T(8,128)S(1)}, f32[80,768]{1,0:T(8,128)S(1)}, u32[]{:S(2)}, u32[]{:S(2)}) collective-permute-start(f32[80,768]{1,0:T(8,128)S(1)} %get-tuple-element.156), channel_id=1, source_target_pairs={{0,2},{2,0},{4,6},{6,4},{1,3},{3,1},{5,7},{7,5},{8,10},{10,8},{12,... | collective-permute-start | bytes 737288 | tf_op jit(solution)/shard_map/ppermute | solution.py:327
  126.2 9.8 %copy-start = (f32[128,768]{1,0:T(8,128)S(1)}, f32[128,768]{1,0:T(8,128)}, u32[]{:S(2)}) copy-start(f32[128,768]{1,0:T(8,128)} %param.7) | copy-start | bytes 1179652
  128.3 10.7 %collective-permute-start.28 = (f32[48,768]{1,0:T(8,128)S(1)}, f32[48,768]{1,0:T(8,128)S(1)}, u32[]{:S(2)}, u32[]{:S(2)}) collective-permute-start(f32[48,768]{1,0:T(8,128)S(1)} %get-tuple-element.170), channel_id=1, source_target_pairs={{0,6},{2,4},{4,2},{6,0},{1,7},{3,5},{5,3},{7,1},{8,14},{10,12},{12... | collective-permute-start | bytes 442376 | tf_op jit(solution)/shard_map/ppermute | solution.py:327
  131.0 10.7 %collective-permute-start.29 = (f32[48,768]{1,0:T(8,128)S(1)}, f32[48,768]{1,0:T(8,128)S(1)}, u32[]{:S(2)}, u32[]{:S(2)}) collective-permute-start(f32[48,768]{1,0:T(8,128)S(1)} %get-tuple-element.171), channel_id=1, source_target_pairs={{0,4},{2,6},{4,0},{6,2},{1,5},{3,7},{5,1},{7,3},{8,12},{10,14},{12... | collective-permute-start | bytes 442376 | tf_op jit(solution)/shard_map/ppermute | solution.py:327
  131.5 10.5 %collective-permute-start.30 = (f32[48,768]{1,0:T(8,128)S(1)}, f32[48,768]{1,0:T(8,128)S(1)}, u32[]{:S(2)}, u32[]{:S(2)}) collective-permute-start(f32[48,768]{1,0:T(8,128)S(1)} %get-tuple-element.172), channel_id=1, source_target_pairs={{0,2},{2,0},{4,6},{6,4},{1,3},{3,1},{5,7},{7,5},{8,10},{10,8},{12,... | collective-permute-start | bytes 442376 | tf_op jit(solution)/shard_map/ppermute | solution.py:327

commit v2 on v1

--- a/solution.py
+++ b/solution.py
@@ -8,8 +8,8 @@
 BLK = 128
 CHUNK = 2
 COST = 20
-SPLIT = 5
-PART_COST = (20, 4)
+PARTS = (0, 4, 6, 8)
+PART_COST = (20, 20, 20)
 DEPTH = 4
 VMEM_LIMIT = 30 * 1024 * 1024
 
@@ -43,8 +43,10 @@
 
 
 def row_range(height, part):
-    first = height * SPLIT // 64 * 8
-    return {None: (0, height), 0: (0, first), 1: (first, height - first)}[part]
+    if part is None:
+        return 0, height
+    low, high = (height * PARTS[i] // 64 * 8 for i in (part, part + 1))
+    return low, high - low
 
 
 def block_copy(t2_ref, number, out, sem, part=None):
@@ -348,10 +350,10 @@
 
     def places(c):
         groups = [[d * cap + j for d, _, j in g] for g in slots(c)] if c <= end else []
-        return [(g, p) for p in ([0, 1] if c == end else [None]) for g in groups]
+        return [(g, p) for p in (range(len(PARTS) - 1) if c == end else [None]) for g in groups]
 
     def send(packed):
-        return [over_slab(x, d) for x, d in zip(packed, [*dists] * 2)]
+        return [over_slab(x, d) for x, d in zip(packed, dists)]
 
     def at_once(arrived, groups):
         return over_rep(jnp.concatenate(arrived, axis=0), [s for g in groups for s in g])
@@ -388,8 +390,9 @@
             cost=COST,
         )
         if c + 1 == end:
-            late, acc = lax.optimization_barrier((late, acc))
-            landed.append(send(late))
+            next_part, acc = lax.optimization_barrier((late[:n], acc))
+            landed.append(send(next_part))
+            late = late[n:]
         if c == 0:
             (acc,) = products(acc, older, cost=0)
         kwargs = {"ready": ready.get(c, (None, None))[1], "turn": c + 1 == end}
@@ -399,7 +402,11 @@
         if c == max(end - 2, 0):
             acc = prepare_ahead(end, acc)
     result = []
-    for part in (0, 1):
+    for part in range(len(PARTS) - 1):
+        if late:
+            next_part, acc = lax.optimization_barrier((late[:n], acc))
+            landed.append(send(next_part))
+            late = late[n:]
         arrived, acc = lax.optimization_barrier((landed[end + part], acc))
         others = at_once(arrived, slots(end))
         first, second = ready[end]
@@ -407,7 +414,7 @@
             None, list(zip(arrived, slots(end))), ready=first, part=part, cost=PART_COST[part]
         )
         sums = products(
-            sums, others, ready=second, base=acc, part=part, cost=COST * (1 - part)
+            sums, others, ready=second, base=acc, part=part, cost=PART_COST[part]
         )
         sums, acc = lax.optimization_barrier((sums, acc))
         low, size = row_range(r_in.shape[0], part)

time: 143 us -> 144 us (level)
  waiting for transfers between devices: 38.8 us -> 30.6 us
  starting transfers between devices: 36.8 us -> 43.8 us
  Pallas kernels: 63.9 us -> 65.7 us
    ppermute x24 -> x30, waiting for transfers between devices: 38.8 us -> 30.4 us  [over_slab(): return lax.ppermute(x, 'slab', [(i, i ^ d) for i in range(slabs)])]
    ppermute x24 -> x30, starting transfers between devices: 35.9 us -> 42.8 us  [over_slab(): return lax.ppermute(x, 'slab', [(i, i ^ d) for i in range(slabs)])]
    pallas_call x14 -> x16, Pallas kernels: 55.6 us -> 57.4 us  [add_products(): pl.pallas_call(body, out_shape=out_shape, in_specs=specs, out_specs=[whol...]
  transfers between devices with their start and end apart: 31 -> 38, of which waited for: 14 -> 12; matrix products, arithmetic and copies ran while one was open for 1% -> 1% of each run, Pallas kernels for 43% -> 44%
where the time goes in v2:
time: 144 us; the launch traced here: 143 us
  Pallas kernels  65.7 us (46%)
  starting transfers between devices  43.8 us (30%)
  waiting for transfers between devices  30.6 us (21%)
  other arithmetic  2.82 us (2%)
    pallas_call x16, Pallas kernels, add_products(): pl.pallas_call(body, out_shape=out_shape, in_specs=specs, out_specs=[whol...  57.4 us
    ppermute x30, starting transfers between devices, over_slab(): return lax.ppermute(x, 'slab', [(i, i ^ d) for i in range(slabs)])  42.8 us
    ppermute x30, waiting for transfers between devices, over_slab(): return lax.ppermute(x, 'slab', [(i, i ^ d) for i in range(slabs)])  30.4 us
    pallas_call x2, Pallas kernels, prepare(): pl.pallas_call(body, out_shape=[jax.ShapeDtypeStruct((cols, 2 * len(g) *...  6.32 us
  transfers between devices with their start and end apart: 38, of which 12 were waited for; matrix products, arithmetic and copies ran while one was open for 1% of the time, Pallas kernels for 44%

profile of v2, /device:TPU:0, one launch (start us, length us, event | category | flops | bytes accessed | tf_op | source)
XLA Modules:
  0.0 143.5 jit_solution(9341741357837507802)
XLA Ops:
  0.0 0.7 fusion.2
  1.1 2.0 %pack.1 = (f32[2,4,128,128]{3,2,1,0:T(8,128)S(1)}, f32[2,4,128,128]{3,2,1,0:T(8,128)S(1)}, f32[2,4,128,128]{3,2,1,0:T(8,128)S(1)}) custom-call(s32[40]{0:T(128)S(1)} %select_reduce_fusion.1.ids.refs_2_, f32[4,128,5120]{2,1,0:T(8,128)} %bitcast.47), custom_call_target="tpu_custom_call" | custom-call | bytes 3145728 | tf_op jit(solution)/shard_map/pack/pallas_call | solution.py:83
  3.1 3.0 %collective-permute-start.1 = (f32[2,512,128]{2,1,0:T(8,128)S(1)}, f32[2,512,128]{2,1,0:T(8,128)S(1)}, u32[]{:S(2)}, u32[]{:S(2)}) collective-permute-start(f32[2,512,128]{2,1,0:T(8,128)S(1)} %bitcast.37), channel_id=1, source_target_pairs={{0,4},{2,6},{4,0},{6,2},{1,5},{3,7},{5,1},{7,3},{8,12},{10,14},{12... | collective-permute-start | bytes 1572872 | tf_op jit(solution)/shard_map/ppermute | solution.py:329
  6.1 1.4 collective-permute-start
  8.1 6.8 %products.16 = (f32[768,512]{1,0:T(8,128)S(1)}, f32[10,4,128,128]{3,2,1,0:T(8,128)S(1)}, f32[2,4,128,128]{3,2,1,0:T(8,128)S(1)}, f32[2,4,128,128]{3,2,1,0:T(8,128)S(1)}, f32[2,4,128,128]{3,2,1,0:T(8,128)S(1)}) custom-call(s32[4,2,10]{2,1,0:T(2,128)S(1)} %reshape.151.refs_0_.refs_1_.ids, s32[4,2,10]{2,1,0:T(2,128)S(1)} %reshape.151.refs_0_.refs_1_.ids, ...), custom_call_target="tpu_custom_call" | custom-call | flops 60397977600 | bytes 193986560 | tf_op jit(solution)/shard_map/products/pallas_call | solution.py:279
  14.8 2.9 %collective-permute-start.6 = (f32[2,512,128]{2,1,0:T(8,128)S(1)}, f32[2,512,128]{2,1,0:T(8,128)S(1)}, u32[]{:S(2)}, u32[]{:S(2)}) collective-permute-start(f32[2,512,128]{2,1,0:T(8,128)S(1)} %bitcast.34), channel_id=1, source_target_pairs={{0,6},{2,4},{4,2},{6,0},{1,7},{3,5},{5,3},{7,1},{8,14},{10,12},{12... | collective-permute-start | bytes 1572872 | tf_op jit(solution)/shard_map/ppermute | solution.py:329
  18.3 12.1 %collective-permute-done.1.refs_8_ = f32[2,512,128]{2,1,0:T(8,128)S(1)} collective-permute-done((f32[2,512,128]{2,1,0:T(8,128)S(1)}, f32[2,512,128]{2,1,0:T(8,128)S(1)}, u32[]{:S(2)}, u32[]{:S(2)}) %collective-permute-start.1) | collective-permute-done | bytes 524320 | tf_op jit(solution)/shard_map/ppermute | solution.py:329
  30.3 2.2 %collective-permute-start.8 = (f32[2,512,128]{2,1,0:T(8,128)S(1)}, f32[2,512,128]{2,1,0:T(8,128)S(1)}, u32[]{:S(2)}, u32[]{:S(2)}) collective-permute-start(f32[2,512,128]{2,1,0:T(8,128)S(1)} %bitcast.31), channel_id=1, source_target_pairs={{0,2},{2,0},{4,6},{6,4},{1,3},{3,1},{5,7},{7,5},{8,10},{10,8},{12,... | collective-permute-start | bytes 1572872 | tf_op jit(solution)/shard_map/ppermute | solution.py:329
  32.7 0.6 collective-permute-start.10
  33.2 4.7 %products.17 = (f32[768,512]{1,0:T(8,128)S(1)}, f32[2,4,128,128]{3,2,1,0:T(8,128)S(1)}, f32[2,4,128,128]{3,2,1,0:T(8,128)S(1)}, f32[2,4,128,128]{3,2,1,0:T(8,128)S(1)}) custom-call(s32[4,2,10]{2,1,0:T(2,128)S(1)} %reshape.151.refs_0_.refs_1_.ids, s32[4,2,10]{2,1,0:T(2,128)S(1)} %reshape.151.refs_0_.refs_1_.ids, s32[40]{0:T(128)S(1)} %select_reduce_fusion.1.ids.refs_2_, ...), custom_call_target="tpu_custom_call" | custom-call | flops 36238786560 | bytes 141557760 | tf_op jit(solution)/shard_map/products/pallas_call | solution.py:279
  37.9 2.6 %collective-permute-start.4 = (f32[2,512,128]{2,1,0:T(8,128)S(1)}, f32[2,512,128]{2,1,0:T(8,128)S(1)}, u32[]{:S(2)}, u32[]{:S(2)}) collective-permute-start(f32[2,512,128]{2,1,0:T(8,128)S(1)} %bitcast.32), channel_id=1, source_target_pairs={{0,4},{2,6},{4,0},{6,2},{1,5},{3,7},{5,1},{7,3},{8,12},{10,14},{12... | collective-permute-start | bytes 1572872 | tf_op jit(solution)/shard_map/ppermute | solution.py:329
  40.5 5.9 %products.18.refs_6_ = f32[768,512]{1,0:T(8,128)S(1)} custom-call(s32[4,2,10]{2,1,0:T(2,128)S(1)} %reshape.151.refs_0_.refs_1_.ids, s32[4,2,10]{2,1,0:T(2,128)S(1)} %reshape.151.refs_0_.refs_1_.ids, s32[40]{0:T(128)S(1)} %select_reduce_fusion.1.ids.refs_2_, s32[2]{0:T(128)S(1)} %pad_add_fusion.refs_3_, f32[768,10240]{1,0:T(8,128)} %refs_4_.31, ...), custom_call_target="tpu_custom_call" | custom-call | tf_op jit(solution)/shard_map/products/pallas_call | solution.py:279
  46.5 4.4 %products.19.refs_6_ = f32[768,512]{1,0:T(8,128)S(1)} custom-call(s32[4,2,10]{2,1,0:T(2,128)S(1)} %reshape.151.refs_0_.refs_1_.ids, s32[4,2,10]{2,1,0:T(2,128)S(1)} %reshape.151.refs_0_.refs_1_.ids, s32[40]{0:T(128)S(1)} %select_reduce_fusion.1.ids.refs_2_, s32[2]{0:T(128)S(1)} %pad_add_fusion.refs_3_, f32[768,10240]{1,0:T(8,128)} %refs_4_.31, ...), custom_call_target="tpu_custom_call" | custom-call | tf_op jit(solution)/shard_map/products/pallas_call | solution.py:279
  50.9 1.5 %collective-permute-start.5 = (f32[2,512,128]{2,1,0:T(8,128)S(1)}, f32[2,512,128]{2,1,0:T(8,128)S(1)}, u32[]{:S(2)}, u32[]{:S(2)}) collective-permute-start(f32[2,512,128]{2,1,0:T(8,128)S(1)} %bitcast.27), channel_id=1, source_target_pairs={{0,2},{2,0},{4,6},{6,4},{1,3},{3,1},{5,7},{7,5},{8,10},{10,8},{12,... | collective-permute-start | bytes 1572872 | tf_op jit(solution)/shard_map/ppermute | solution.py:329
  52.8 1.5 %collective-permute-done.8.refs_9_ = f32[2,512,128]{2,1,0:T(8,128)S(1)} collective-permute-done((f32[2,512,128]{2,1,0:T(8,128)S(1)}, f32[2,512,128]{2,1,0:T(8,128)S(1)}, u32[]{:S(2)}, u32[]{:S(2)}) %collective-permute-start.8) | collective-permute-done | bytes 524320 | tf_op jit(solution)/shard_map/ppermute | solution.py:329
  54.4 4.9 %products.20 = (f32[768,512]{1,0:T(8,128)S(1)}, f32[2,4,128,128]{3,2,1,0:T(8,128)S(1)}, f32[2,4,128,128]{3,2,1,0:T(8,128)S(1)}, f32[2,4,128,128]{3,2,1,0:T(8,128)S(1)}) custom-call(s32[4,2,10]{2,1,0:T(2,128)S(1)} %reshape.151.refs_0_.refs_1_.ids, s32[4,2,10]{2,1,0:T(2,128)S(1)} %reshape.151.refs_0_.refs_1_.ids, s32[40]{0:T(128)S(1)} %select_reduce_fusion.1.ids.refs_2_, ...), custom_call_target="tpu_custom_call" | custom-call | flops 36238786560 | bytes 141557760 | tf_op jit(solution)/shard_map/products/pallas_call | solution.py:279
  59.3 3.0 %collective-permute-start.16 = (f32[2,512,128]{2,1,0:T(8,128)S(1)}, f32[2,512,128]{2,1,0:T(8,128)S(1)}, u32[]{:S(2)}, u32[]{:S(2)}) collective-permute-start(f32[2,512,128]{2,1,0:T(8,128)S(1)} %bitcast.30), channel_id=1, source_target_pairs={{0,6},{2,4},{4,2},{6,0},{1,7},{3,5},{5,3},{7,1},{8,14},{10,12},{12... | collective-permute-start | bytes 1572872 | tf_op jit(solution)/shard_map/ppermute | solution.py:329
  62.3 0.5 collective-permute-start.17
  62.8 4.4 %products.21.refs_6_ = f32[768,512]{1,0:T(8,128)S(1)} custom-call(s32[4,2,10]{2,1,0:T(2,128)S(1)} %reshape.151.refs_0_.refs_1_.ids, s32[4,2,10]{2,1,0:T(2,128)S(1)} %reshape.151.refs_0_.refs_1_.ids, s32[40]{0:T(128)S(1)} %select_reduce_fusion.1.ids.refs_2_, s32[2]{0:T(128)S(1)} %pad_add_fusion.refs_3_, f32[768,10240]{1,0:T(8,128)} %refs_4_.31, ...), custom_call_target="tpu_custom_call" | custom-call | tf_op jit(solution)/shard_map/products/pallas_call | solution.py:279
  67.2 3.2 %prepare.2 = (bf16[768,1536]{1,0:T(8,128)(2,1)S(1)}, bf16[768,1536]{1,0:T(8,128)(2,1)S(1)}) custom-call(s32[4,2,10]{2,1,0:T(2,128)S(1)} %reshape.151.refs_0_.refs_1_.ids, f32[768,10240]{1,0:T(8,128)} %refs_4_.31), custom_call_target="tpu_custom_call" | custom-call | bytes 9437184 | tf_op jit(solution)/shard_map/prepare/pallas_call | solution.py:138
  70.3 4.9 %collective-permute-done.4.refs_8_ = f32[2,512,128]{2,1,0:T(8,128)S(1)} collective-permute-done((f32[2,512,128]{2,1,0:T(8,128)S(1)}, f32[2,512,128]{2,1,0:T(8,128)S(1)}, u32[]{:S(2)}, u32[]{:S(2)}) %collective-permute-start.4) | collective-permute-done | bytes 524320 | tf_op jit(solution)/shard_map/ppermute | solution.py:329
  75.2 2.2 %collective-permute-start.18 = (f32[2,512,128]{2,1,0:T(8,128)S(1)}, f32[2,512,128]{2,1,0:T(8,128)S(1)}, u32[]{:S(2)}, u32[]{:S(2)}) collective-permute-start(f32[2,512,128]{2,1,0:T(8,128)S(1)} %bitcast.26), channel_id=1, source_target_pairs={{0,2},{2,0},{4,6},{6,4},{1,3},{3,1},{5,7},{7,5},{8,10},{10,8},{12,... | collective-permute-start | bytes 1572872 | tf_op jit(solution)/shard_map/ppermute | solution.py:329
  77.6 4.6 %products.22 = (f32[768,512]{1,0:T(8,128)S(1)}, f32[2,4,64,128]{3,2,1,0:T(8,128)S(1)}, f32[2,4,64,128]{3,2,1,0:T(8,128)S(1)}, f32[2,4,64,128]{3,2,1,0:T(8,128)S(...) custom-call(s32[4,2,10]{2,1,0:T(2,128)S(1)} %reshape.151.refs_0_.ref, ...), custom_call_target="tpu_custom_call" | custom-call | flops 36238786560 | bytes 141557760 | tf_op jit(solution)/shard_map/products/pallas_call | solution.py:279
  82.2 2.3 %collective-permute-start.13 = (f32[2,256,128]{2,1,0:T(8,128)S(1)}, f32[2,256,128]{2,1,0:T(8,128)S(1)}, u32[]{:S(2)}, u32[]{:S(2)}) collective-permute-start(f32[2,256,128]{2,1,0:T(8,128)S(1)} %bitcast.40), channel_id=1, source_target_pairs={{0,6},{2,4},{4,2},{6,0},{1,7},{3,5},{5,3},{7,1},{8,14},{10,12},{12... | collective-permute-start | bytes 786440 | tf_op jit(solution)/shard_map/ppermute | solution.py:329
  85.0 4.4 %products.23.refs_6_ = f32[768,512]{1,0:T(8,128)S(1)} custom-call(s32[4,2,10]{2,1,0:T(2,128)S(1)} %reshape.151.refs_0_.refs_1_.ids, s32[4,2,10]{2,1,0:T(2,128)S(1)} %reshape.151.refs_0_.refs_1_.ids, s32[40]{0:T(128)S(1)} %select_reduce_fusion.1.ids.refs_2_, s32[2]{0:T(128)S(1)} %pad_add_fusion.refs_3_, f32[768,10240]{1,0:T(8,128)} %refs_4_.31, ...), custom_call_target="tpu_custom_call" | custom-call | tf_op jit(solution)/shard_map/products/pallas_call | solution.py:279
  89.4 3.2 %prepare.3 = (bf16[768,1536]{1,0:T(8,128)(2,1)S(1)}, bf16[768,1536]{1,0:T(8,128)(2,1)S(1)}) custom-call(s32[4,2,10]{2,1,0:T(2,128)S(1)} %reshape.151.refs_0_.refs_1_.ids, f32[768,10240]{1,0:T(8,128)} %refs_4_.31), custom_call_target="tpu_custom_call" | custom-call | bytes 9437184 | tf_op jit(solution)/shard_map/prepare/pallas_call | solution.py:138
  92.6 1.3 collective-permute-start.15
  93.9 3.8 %collective-permute-done.17.refs_9_ = f32[2,512,128]{2,1,0:T(8,128)S(1)} collective-permute-done((f32[2,512,128]{2,1,0:T(8,128)S(1)}, f32[2,512,128]{2,1,0:T(8,128)S(1)}, u32[]{:S(2)}, u32[]{:S(2)}) %collective-permute-start.17) | collective-permute-done | bytes 524320 | tf_op jit(solution)/shard_map/ppermute | solution.py:329
  97.6 1.6 %collective-permute-done.18.refs_10_ = f32[2,512,128]{2,1,0:T(8,128)S(1)} collective-permute-done((f32[2,512,128]{2,1,0:T(8,128)S(1)}, f32[2,512,128]{2,1,0:T(8,128)S(1)}, u32[]{:S(2)}, u32[]{:S(2)}) %collective-permute-start.18) | collective-permute-done | bytes 524320 | tf_op jit(solution)/shard_map/ppermute | solution.py:329
  99.4 2.8 %products.24.refs_6_ = f32[768,512]{1,0:T(8,128)S(1)} custom-call(s32[4,2,10]{2,1,0:T(2,128)S(1)} %reshape.151.refs_0_.refs_1_.ids, s32[4,2,10]{2,1,0:T(2,128)S(1)} %reshape.151.refs_0_.refs_1_.ids, s32[40]{0:T(128)S(1)} %select_reduce_fusion.1.ids.refs_2_, s32[2]{0:T(128)S(1)} %pad_add_fusion.refs_3_, f32[768,10240]{1,0:T(8,128)} %refs_4_.31, ...), custom_call_target="tpu_custom_call" | custom-call | flops 36238786560 | bytes 141557760 | tf_op jit(solution)/shard_map/products/pallas_call | solution.py:279
  102.2 3.0 %collective-permute-start.24 = (f32[2,128,128]{2,1,0:T(8,128)S(1)}, f32[2,128,128]{2,1,0:T(8,128)S(1)}, u32[]{:S(2)}, u32[]{:S(2)}) collective-permute-start(f32[2,128,128]{2,1,0:T(8,128)S(1)} %bitcast.46), channel_id=1, source_target_pairs={{0,6},{2,4},{4,2},{6,0},{1,7},{3,5},{5,3},{7,1},{8,14},{10,12},{12... | collective-permute-start | bytes 393224 | tf_op jit(solution)/shard_map/ppermute | solution.py:329
  105.7 3.1 %products.25.refs_7_ = f32[512,768]{1,0:T(8,128)S(1)} custom-call(s32[4,2,10]{2,1,0:T(2,128)S(1)} %reshape.151.refs_0_.refs_1_.ids, s32[4,2,10]{2,1,0:T(2,128)S(1)} %reshape.151.refs_0_.refs_1_.ids, s32[40]{0:T(128)S(1)} %select_reduce_fusion.1.ids.refs_2_, s32[2]{0:T(128)S(1)} %pad_add_fusion.refs_3_, f32[768,10240]{1,0:T(8,128)} %refs_4_.31, ...), custom_call_target="tpu_custom_call" | custom-call | tf_op jit(solution)/shard_map/products/pallas_call | solution.py:279
  108.8 0.7 collective-permute-start.26
  109.4 1.1 collective-permute-done.15.refs_9_
  110.5 2.9 %collective-permute-start.31 = (f32[2,128,128]{2,1,0:T(8,128)S(1)}, f32[2,128,128]{2,1,0:T(8,128)S(1)}, u32[]{:S(2)}, u32[]{:S(2)}) collective-permute-start(f32[2,128,128]{2,1,0:T(8,128)S(1)} %bitcast.43), channel_id=1, source_target_pairs={{0,6},{2,4},{4,2},{6,0},{1,7},{3,5},{5,3},{7,1},{8,14},{10,12},{12... | collective-permute-start | bytes 393224 | tf_op jit(solution)/shard_map/ppermute | solution.py:329
  113.6 2.1 %products.26.refs_6_ = f32[768,256]{1,0:T(8,128)S(1)} custom-call(s32[4,2,10]{2,1,0:T(2,128)S(1)} %reshape.151.refs_0_.refs_1_.ids, s32[4,2,10]{2,1,0:T(2,128)S(1)} %reshape.151.refs_0_.refs_1_.ids, s32[40]{0:T(128)S(1)} %select_reduce_fusion.1.ids.refs_2_, s32[2]{0:T(128)S(1)} %pad_add_fusion.refs_3_, f32[768,10240]{1,0:T(8,128)} %refs_4_.31, ...), custom_call_target="tpu_custom_call" | custom-call | flops 18119393280 | bytes 94371840 | tf_op jit(solution)/shard_map/products/pallas_call | solution.py:279
  115.8 0.5 collective-permute-start.32
  116.4 2.0 %products.27 = (f32[64,768]{1,0:T(8,128)S(1)}, f32[64,768]{1,0:T(8,128)S(1)}, f32[64,768]{1,0:T(8,128)S(1)}, f32[64,768]{1,0:T(8,128)S(1)}) custom-call(s32[4,2,10]{2,1,0:T(2,128)S(1)} %reshape.151.refs_0_.refs_1_.ids, s32[4,2,10]{2,1,0:T(2,128)S(1)} %reshape.151.refs_0_.refs_1_.ids, s32[40]{0:T(128)S(1)} %select_reduce_fusion.1.ids.refs_2_, ...), custom_call_target="tpu_custom_call" | custom-call | flops 18119393280 | bytes 94371840 | tf_op jit(solution)/shard_map/products/pallas_call | solution.py:279
  118.7 1.8 %products.28.refs_6_ = f32[768,128]{1,0:T(8,128)S(1)} custom-call(s32[4,2,10]{2,1,0:T(2,128)S(1)} %reshape.151.refs_0_.refs_1_.ids, s32[4,2,10]{2,1,0:T(2,128)S(1)} %reshape.151.refs_0_.refs_1_.ids, s32[40]{0:T(128)S(1)} %select_reduce_fusion.1.ids.refs_2_, s32[2]{0:T(128)S(1)} %pad_add_fusion.refs_3_, f32[768,10240]{1,0:T(8,128)} %refs_4_.31, ...), custom_call_target="tpu_custom_call" | custom-call | flops 9059696640 | bytes 70778880 | tf_op jit(solution)/shard_map/products/pallas_call | solution.py:279
  120.5 3.0 %collective-permute-start.21 = (f32[64,768]{1,0:T(8,128)S(1)}, f32[64,768]{1,0:T(8,128)S(1)}, u32[]{:S(2)}, u32[]{:S(2)}) collective-permute-start(f32[64,768]{1,0:T(8,128)S(1)} %get-tuple-element.178), channel_id=1, source_target_pairs={{0,6},{2,4},{4,2},{6,0},{1,7},{3,5},{5,3},{7,1},{8,14},{10,12},{12... | collective-permute-start | bytes 589832 | tf_op jit(solution)/shard_map/ppermute | solution.py:329
  124.0 2.0 %products.29 = (f32[32,768]{1,0:T(8,128)S(1)}, f32[32,768]{1,0:T(8,128)S(1)}, f32[32,768]{1,0:T(8,128)S(1)}, f32[32,768]{1,0:T(8,128)S(1)}) custom-call(s32[4,2,10]{2,1,0:T(2,128)S(1)} %reshape.151.refs_0_.refs_1_.ids, s32[4,2,10]{2,1,0:T(2,128)S(1)} %reshape.151.refs_0_.refs_1_.ids, s32[40]{0:T(128)S(1)} %select_reduce_fusion.1.ids.refs_2_, ...), custom_call_target="tpu_custom_call" | custom-call | flops 9059696640 | bytes 70778880 | tf_op jit(solution)/shard_map/products/pallas_call | solution.py:279
  126.3 1.8 %products.30.refs_6_ = f32[768,128]{1,0:T(8,128)S(1)} custom-call(s32[4,2,10]{2,1,0:T(2,128)S(1)} %reshape.151.refs_0_.refs_1_.ids, s32[4,2,10]{2,1,0:T(2,128)S(1)} %reshape.151.refs_0_.refs_1_.ids, s32[40]{0:T(128)S(1)} %select_reduce_fusion.1.ids.refs_2_, s32[2]{0:T(128)S(1)} %pad_add_fusion.refs_3_, f32[768,10240]{1,0:T(8,128)} %refs_4_.31, ...), custom_call_target="tpu_custom_call" | custom-call | flops 9059696640 | bytes 70778880 | tf_op jit(solution)/shard_map/products/pallas_call | solution.py:279
  128.2 2.9 %collective-permute-start.28 = (f32[32,768]{1,0:T(8,128)S(1)}, f32[32,768]{1,0:T(8,128)S(1)}, u32[]{:S(2)}, u32[]{:S(2)}) collective-permute-start(f32[32,768]{1,0:T(8,128)S(1)} %get-tuple-element.194), channel_id=1, source_target_pairs={{0,6},{2,4},{4,2},{6,0},{1,7},{3,5},{5,3},{7,1},{8,14},{10,12},{12... | collective-permute-start | bytes 294920 | tf_op jit(solution)/shard_map/ppermute | solution.py:329
  131.6 2.0 %products.31 = (f32[32,768]{1,0:T(8,128)S(1)}, f32[32,768]{1,0:T(8,128)S(1)}, f32[32,768]{1,0:T(8,128)S(1)}, f32[32,768]{1,0:T(8,128)S(1)}) custom-call(s32[4,2,10]{2,1,0:T(2,128)S(1)} %reshape.151.refs_0_.refs_1_.ids, s32[4,2,10]{2,1,0:T(2,128)S(1)} %reshape.151.refs_0_.refs_1_.ids, s32[40]{0:T(128)S(1)} %select_reduce_fusion.1.ids.refs_2_, ...), custom_call_target="tpu_custom_call" | custom-call | flops 9059696640 | bytes 70778880 | tf_op jit(solution)/shard_map/products/pallas_call | solution.py:279
  134.0 2.6 %collective-permute-start.35 = (f32[32,768]{1,0:T(8,128)S(1)}, f32[32,768]{1,0:T(8,128)S(1)}, u32[]{:S(2)}, u32[]{:S(2)}) collective-permute-start(f32[32,768]{1,0:T(8,128)S(1)} %get-tuple-element.210), channel_id=1, source_target_pairs={{0,6},{2,4},{4,2},{6,0},{1,7},{3,5},{5,3},{7,1},{8,14},{10,12},{12... | collective-permute-start | bytes 294920 | tf_op jit(solution)/shard_map/ppermute | solution.py:329
  137.6 1.5 %collective-permute-done.30 = f32[32,768]{1,0:T(8,128)S(1)} collective-permute-done((f32[32,768]{1,0:T(8,128)S(1)}, f32[32,768]{1,0:T(8,128)S(1)}, u32[]{:S(2)}, u32[]{:S(2)}) %collective-permute-start.30) | collective-permute-done | bytes 98336 | tf_op jit(solution)/shard_map/ppermute | solution.py:329
  139.2 3.2 %collective-permute-done.35 = f32[32,768]{1,0:T(8,128)S(1)} collective-permute-done((f32[32,768]{1,0:T(8,128)S(1)}, f32[32,768]{1,0:T(8,128)S(1)}, u32[]{:S(2)}, u32[]{:S(2)}) %collective-permute-start.35) | collective-permute-done | bytes 98336 | tf_op jit(solution)/shard_map/ppermute | solution.py:329
  142.7 0.8 pad_maximum_fusion.7
  (68 shorter events, 7.1 us)
Async XLA Ops:
  3.1 27.2 %collective-permute-start.1 = (f32[2,512,128]{2,1,0:T(8,128)S(1)}, f32[2,512,128]{2,1,0:T(8,128)S(1)}, u32[]{:S(2)}, u32[]{:S(2)}) collective-permute-start(f32[2,512,128]{2,1,0:T(8,128)S(1)} %bitcast.37), channel_id=1, source_target_pairs={{0,4},{2,6},{4,0},{6,2},{1,5},{3,7},{5,1},{7,3},{8,12},{10,14},{12... | collective-permute-start | bytes 1572872 | tf_op jit(solution)/shard_map/ppermute | solution.py:329
  6.1 26.4 %collective-permute-start = (f32[2,512,128]{2,1,0:T(8,128)S(1)}, f32[2,512,128]{2,1,0:T(8,128)S(1)}, u32[]{:S(2)}, u32[]{:S(2)}) collective-permute-start(f32[2,512,128]{2,1,0:T(8,128)S(1)} %bitcast.36), channel_id=1, source_target_pairs={{0,6},{2,4},{4,2},{6,0},{1,7},{3,5},{5,3},{7,1},{8,14},{10,12},{12... | collective-permute-start | bytes 1572872 | tf_op jit(solution)/shard_map/ppermute | solution.py:329
  7.6 25.0 %collective-permute-start.2 = (f32[2,512,128]{2,1,0:T(8,128)S(1)}, f32[2,512,128]{2,1,0:T(8,128)S(1)}, u32[]{:S(2)}, u32[]{:S(2)}) collective-permute-start(f32[2,512,128]{2,1,0:T(8,128)S(1)} %bitcast.35), channel_id=1, source_target_pairs={{0,2},{2,0},{4,6},{6,4},{1,3},{3,1},{5,7},{7,5},{8,10},{10,8},{12,... | collective-permute-start | bytes 1572872 | tf_op jit(solution)/shard_map/ppermute | solution.py:329
  14.8 36.1 %collective-permute-start.6 = (f32[2,512,128]{2,1,0:T(8,128)S(1)}, f32[2,512,128]{2,1,0:T(8,128)S(1)}, u32[]{:S(2)}, u32[]{:S(2)}) collective-permute-start(f32[2,512,128]{2,1,0:T(8,128)S(1)} %bitcast.34), channel_id=1, source_target_pairs={{0,6},{2,4},{4,2},{6,0},{1,7},{3,5},{5,3},{7,1},{8,14},{10,12},{12... | collective-permute-start | bytes 1572872 | tf_op jit(solution)/shard_map/ppermute | solution.py:329
  17.8 35.0 %collective-permute-start.7 = (f32[2,512,128]{2,1,0:T(8,128)S(1)}, f32[2,512,128]{2,1,0:T(8,128)S(1)}, u32[]{:S(2)}, u32[]{:S(2)}) collective-permute-start(f32[2,512,128]{2,1,0:T(8,128)S(1)} %bitcast.33), channel_id=1, source_target_pairs={{0,4},{2,6},{4,0},{6,2},{1,5},{3,7},{5,1},{7,3},{8,12},{10,14},{12... | collective-permute-start | bytes 1572872 | tf_op jit(solution)/shard_map/ppermute | solution.py:329
  30.3 23.9 %collective-permute-start.8 = (f32[2,512,128]{2,1,0:T(8,128)S(1)}, f32[2,512,128]{2,1,0:T(8,128)S(1)}, u32[]{:S(2)}, u32[]{:S(2)}) collective-permute-start(f32[2,512,128]{2,1,0:T(8,128)S(1)} %bitcast.31), channel_id=1, source_target_pairs={{0,2},{2,0},{4,6},{6,4},{1,3},{3,1},{5,7},{7,5},{8,10},{10,8},{12,... | collective-permute-start | bytes 1572872 | tf_op jit(solution)/shard_map/ppermute | solution.py:329
  32.6 5.4 %collective-permute-start.9 = (f32[10,512,128]{2,1,0:T(8,128)S(1)}, f32[10,512,128]{2,1,0:T(8,128)S(1)}, u32[]{:S(2)}, u32[]{:S(2)}) collective-permute-start(f32[10,512,128]{2,1,0:T(8,128)S(1)} %bitcast.25), channel_id=1, source_target_pairs={{0,1},{1,0},{2,3},{3,2},{4,5},{5,4},{6,7},{7,6},{8,9},{9,8},{10,11... | collective-permute-start | bytes 7864328 | tf_op jit(solution)/shard_map/ppermute | solution.py:334
  32.7 13.8 %collective-permute-start.10 = (f32[6,512,128]{2,1,0:T(8,128)S(1)}, f32[6,512,128]{2,1,0:T(8,128)S(1)}, u32[]{:S(2)}, u32[]{:S(2)}) collective-permute-start(f32[6,512,128]{2,1,0:T(8,128)S(1)} %pad_maximum_fusion), channel_id=1, source_target_pairs={{0,1},{1,0},{2,3},{3,2},{4,5},{5,4},{6,7},{7,6},{8,9},{9,8},{10,11... | collective-permute-start | bytes 4718600 | tf_op jit(solution)/shard_map/ppermute | solution.py:334
  37.9 37.2 %collective-permute-start.4 = (f32[2,512,128]{2,1,0:T(8,128)S(1)}, f32[2,512,128]{2,1,0:T(8,128)S(1)}, u32[]{:S(2)}, u32[]{:S(2)}) collective-permute-start(f32[2,512,128]{2,1,0:T(8,128)S(1)} %bitcast.32), channel_id=1, source_target_pairs={{0,4},{2,6},{4,0},{6,2},{1,5},{3,7},{5,1},{7,3},{8,12},{10,14},{12... | collective-permute-start | bytes 1572872 | tf_op jit(solution)/shard_map/ppermute | solution.py:329
  46.4 31.0 %collective-permute-start.3 = (f32[2,512,128]{2,1,0:T(8,128)S(1)}, f32[2,512,128]{2,1,0:T(8,128)S(1)}, u32[]{:S(2)}, u32[]{:S(2)}) collective-permute-start(f32[2,512,128]{2,1,0:T(8,128)S(1)} %bitcast.29), channel_id=1, source_target_pairs={{0,6},{2,4},{4,2},{6,0},{1,7},{3,5},{5,3},{7,1},{8,14},{10,12},{12... | collective-permute-start | bytes 1572872 | tf_op jit(solution)/shard_map/ppermute | solution.py:329
  50.9 26.5 %collective-permute-start.5 = (f32[2,512,128]{2,1,0:T(8,128)S(1)}, f32[2,512,128]{2,1,0:T(8,128)S(1)}, u32[]{:S(2)}, u32[]{:S(2)}) collective-permute-start(f32[2,512,128]{2,1,0:T(8,128)S(1)} %bitcast.27), channel_id=1, source_target_pairs={{0,2},{2,0},{4,6},{6,4},{1,3},{3,1},{5,7},{7,5},{8,10},{10,8},{12,... | collective-permute-start | bytes 1572872 | tf_op jit(solution)/shard_map/ppermute | solution.py:329
  54.3 7.9 %collective-permute-start.11 = (f32[6,512,128]{2,1,0:T(8,128)S(1)}, f32[6,512,128]{2,1,0:T(8,128)S(1)}, u32[]{:S(2)}, u32[]{:S(2)}) collective-permute-start(f32[6,512,128]{2,1,0:T(8,128)S(1)} %pad_maximum_fusion.1), channel_id=1, source_target_pairs={{0,1},{1,0},{2,3},{3,2},{4,5},{5,4},{6,7},{7,6},{8,9},{9,8},{10,11... | collective-permute-start | bytes 4718600 | tf_op jit(solution)/shard_map/ppermute | solution.py:334
  59.3 33.3 %collective-permute-start.16 = (f32[2,512,128]{2,1,0:T(8,128)S(1)}, f32[2,512,128]{2,1,0:T(8,128)S(1)}, u32[]{:S(2)}, u32[]{:S(2)}) collective-permute-start(f32[2,512,128]{2,1,0:T(8,128)S(1)} %bitcast.30), channel_id=1, source_target_pairs={{0,6},{2,4},{4,2},{6,0},{1,7},{3,5},{5,3},{7,1},{8,14},{10,12},{12... | collective-permute-start | bytes 1572872 | tf_op jit(solution)/shard_map/ppermute | solution.py:329
  62.3 35.4 %collective-permute-start.17 = (f32[2,512,128]{2,1,0:T(8,128)S(1)}, f32[2,512,128]{2,1,0:T(8,128)S(1)}, u32[]{:S(2)}, u32[]{:S(2)}) collective-permute-start(f32[2,512,128]{2,1,0:T(8,128)S(1)} %bitcast.28), channel_id=1, source_target_pairs={{0,4},{2,6},{4,0},{6,2},{1,5},{3,7},{5,1},{7,3},{8,12},{10,14},{12... | collective-permute-start | bytes 1572872 | tf_op jit(solution)/shard_map/ppermute | solution.py:329
  75.2 24.1 %collective-permute-start.18 = (f32[2,512,128]{2,1,0:T(8,128)S(1)}, f32[2,512,128]{2,1,0:T(8,128)S(1)}, u32[]{:S(2)}, u32[]{:S(2)}) collective-permute-start(f32[2,512,128]{2,1,0:T(8,128)S(1)} %bitcast.26), channel_id=1, source_target_pairs={{0,2},{2,0},{4,6},{6,4},{1,3},{3,1},{5,7},{7,5},{8,10},{10,8},{12,... | collective-permute-start | bytes 1572872 | tf_op jit(solution)/shard_map/ppermute | solution.py:329
  77.5 7.0 %collective-permute-start.12 = (f32[6,512,128]{2,1,0:T(8,128)S(1)}, f32[6,512,128]{2,1,0:T(8,128)S(1)}, u32[]{:S(2)}, u32[]{:S(2)}) collective-permute-start(f32[6,512,128]{2,1,0:T(8,128)S(1)} %pad_maximum_fusion.2), channel_id=1, source_target_pairs={{0,1},{1,0},{2,3},{3,2},{4,5},{5,4},{6,7},{7,6},{8,9},{9,8},{10,11... | collective-permute-start | bytes 4718600 | tf_op jit(solution)/shard_map/ppermute | solution.py:334
  82.2 26.6 %collective-permute-start.13 = (f32[2,256,128]{2,1,0:T(8,128)S(1)}, f32[2,256,128]{2,1,0:T(8,128)S(1)}, u32[]{:S(2)}, u32[]{:S(2)}) collective-permute-start(f32[2,256,128]{2,1,0:T(8,128)S(1)} %bitcast.40), channel_id=1, source_target_pairs={{0,6},{2,4},{4,2},{6,0},{1,7},{3,5},{5,3},{7,1},{8,14},{10,12},{12... | collective-permute-start | bytes 786440 | tf_op jit(solution)/shard_map/ppermute | solution.py:329
  84.5 25.0 %collective-permute-start.14 = (f32[2,256,128]{2,1,0:T(8,128)S(1)}, f32[2,256,128]{2,1,0:T(8,128)S(1)}, u32[]{:S(2)}, u32[]{:S(2)}) collective-permute-start(f32[2,256,128]{2,1,0:T(8,128)S(1)} %bitcast.39), channel_id=1, source_target_pairs={{0,4},{2,6},{4,0},{6,2},{1,5},{3,7},{5,1},{7,3},{8,12},{10,14},{12... | collective-permute-start | bytes 786440 | tf_op jit(solution)/shard_map/ppermute | solution.py:329
  92.6 18.0 %collective-permute-start.15 = (f32[2,256,128]{2,1,0:T(8,128)S(1)}, f32[2,256,128]{2,1,0:T(8,128)S(1)}, u32[]{:S(2)}, u32[]{:S(2)}) collective-permute-start(f32[2,256,128]{2,1,0:T(8,128)S(1)} %bitcast.38), channel_id=1, source_target_pairs={{0,2},{2,0},{4,6},{6,4},{1,3},{3,1},{5,7},{7,5},{8,10},{10,8},{12,... | collective-permute-start | bytes 786440 | tf_op jit(solution)/shard_map/ppermute | solution.py:329
  99.4 5.9 %collective-permute-start.19 = (f32[6,512,128]{2,1,0:T(8,128)S(1)}, f32[6,512,128]{2,1,0:T(8,128)S(1)}, u32[]{:S(2)}, u32[]{:S(2)}) collective-permute-start(f32[6,512,128]{2,1,0:T(8,128)S(1)} %pad_maximum_fusion.3), channel_id=1, source_target_pairs={{0,1},{1,0},{2,3},{3,2},{4,5},{5,4},{6,7},{7,6},{8,9},{9,8},{10,11... | collective-permute-start | bytes 4718600 | tf_op jit(solution)/shard_map/ppermute | solution.py:334
  102.2 16.2 %collective-permute-start.24 = (f32[2,128,128]{2,1,0:T(8,128)S(1)}, f32[2,128,128]{2,1,0:T(8,128)S(1)}, u32[]{:S(2)}, u32[]{:S(2)}) collective-permute-start(f32[2,128,128]{2,1,0:T(8,128)S(1)} %bitcast.46), channel_id=1, source_target_pairs={{0,6},{2,4},{4,2},{6,0},{1,7},{3,5},{5,3},{7,1},{8,14},{10,12},{12... | collective-permute-start | bytes 393224 | tf_op jit(solution)/shard_map/ppermute | solution.py:329
  105.2 13.4 %collective-permute-start.25 = (f32[2,128,128]{2,1,0:T(8,128)S(1)}, f32[2,128,128]{2,1,0:T(8,128)S(1)}, u32[]{:S(2)}, u32[]{:S(2)}) collective-permute-start(f32[2,128,128]{2,1,0:T(8,128)S(1)} %bitcast.45), channel_id=1, source_target_pairs={{0,4},{2,6},{4,0},{6,2},{1,5},{3,7},{5,1},{7,3},{8,12},{10,14},{12... | collective-permute-start | bytes 393224 | tf_op jit(solution)/shard_map/ppermute | solution.py:329
  108.8 9.8 %collective-permute-start.26 = (f32[2,128,128]{2,1,0:T(8,128)S(1)}, f32[2,128,128]{2,1,0:T(8,128)S(1)}, u32[]{:S(2)}, u32[]{:S(2)}) collective-permute-start(f32[2,128,128]{2,1,0:T(8,128)S(1)} %bitcast.44), channel_id=1, source_target_pairs={{0,2},{2,0},{4,6},{6,4},{1,3},{3,1},{5,7},{7,5},{8,10},{10,8},{12,... | collective-permute-start | bytes 393224 | tf_op jit(solution)/shard_map/ppermute | solution.py:329
  110.5 15.4 %collective-permute-start.31 = (f32[2,128,128]{2,1,0:T(8,128)S(1)}, f32[2,128,128]{2,1,0:T(8,128)S(1)}, u32[]{:S(2)}, u32[]{:S(2)}) collective-permute-start(f32[2,128,128]{2,1,0:T(8,128)S(1)} %bitcast.43), channel_id=1, source_target_pairs={{0,6},{2,4},{4,2},{6,0},{1,7},{3,5},{5,3},{7,1},{8,14},{10,12},{12... | collective-permute-start | bytes 393224 | tf_op jit(solution)/shard_map/ppermute | solution.py:329
  113.5 2.4 %collective-permute-start.20 = (f32[6,256,128]{2,1,0:T(8,128)S(1)}, f32[6,256,128]{2,1,0:T(8,128)S(1)}, u32[]{:S(2)}, u32[]{:S(2)}) collective-permute-start(f32[6,256,128]{2,1,0:T(8,128)S(1)} %pad_maximum_fusion.4), channel_id=1, source_target_pairs={{0,1},{1,0},{2,3},{3,2},{4,5},{5,4},{6,7},{7,6},{8,9},{9,8},{10,11... | collective-permute-start | bytes 2359304 | tf_op jit(solution)/shard_map/ppermute | solution.py:334
  115.8 10.4 %collective-permute-start.32 = (f32[2,128,128]{2,1,0:T(8,128)S(1)}, f32[2,128,128]{2,1,0:T(8,128)S(1)}, u32[]{:S(2)}, u32[]{:S(2)}) collective-permute-start(f32[2,128,128]{2,1,0:T(8,128)S(1)} %bitcast.42), channel_id=1, source_target_pairs={{0,4},{2,6},{4,0},{6,2},{1,5},{3,7},{5,1},{7,3},{8,12},{10,14},{12... | collective-permute-start | bytes 393224 | tf_op jit(solution)/shard_map/ppermute | solution.py:329
  118.4 7.8 %collective-permute-start.33 = (f32[2,128,128]{2,1,0:T(8,128)S(1)}, f32[2,128,128]{2,1,0:T(8,128)S(1)}, u32[]{:S(2)}, u32[]{:S(2)}) collective-permute-start(f32[2,128,128]{2,1,0:T(8,128)S(1)} %bitcast.41), channel_id=1, source_target_pairs={{0,2},{2,0},{4,6},{6,4},{1,3},{3,1},{5,7},{7,5},{8,10},{10,8},{12,... | collective-permute-start | bytes 393224 | tf_op jit(solution)/shard_map/ppermute | solution.py:329
  118.6 4.9 %collective-permute-start.27 = (f32[6,128,128]{2,1,0:T(8,128)S(1)}, f32[6,128,128]{2,1,0:T(8,128)S(1)}, u32[]{:S(2)}, u32[]{:S(2)}) collective-permute-start(f32[6,128,128]{2,1,0:T(8,128)S(1)} %pad_maximum_fusion.5), channel_id=1, source_target_pairs={{0,1},{1,0},{2,3},{3,2},{4,5},{5,4},{6,7},{7,6},{8,9},{9,8},{10,11... | collective-permute-start | bytes 1179656 | tf_op jit(solution)/shard_map/ppermute | solution.py:334
  120.5 13.0 %collective-permute-start.21 = (f32[64,768]{1,0:T(8,128)S(1)}, f32[64,768]{1,0:T(8,128)S(1)}, u32[]{:S(2)}, u32[]{:S(2)}) collective-permute-start(f32[64,768]{1,0:T(8,128)S(1)} %get-tuple-element.178), channel_id=1, source_target_pairs={{0,6},{2,4},{4,2},{6,0},{1,7},{3,5},{5,3},{7,1},{8,14},{10,12},{12... | collective-permute-start | bytes 589832 | tf_op jit(solution)/shard_map/ppermute | solution.py:329
  123.5 10.5 %collective-permute-start.22 = (f32[64,768]{1,0:T(8,128)S(1)}, f32[64,768]{1,0:T(8,128)S(1)}, u32[]{:S(2)}, u32[]{:S(2)}) collective-permute-start(f32[64,768]{1,0:T(8,128)S(1)} %get-tuple-element.179), channel_id=1, source_target_pairs={{0,4},{2,6},{4,0},{6,2},{1,5},{3,7},{5,1},{7,3},{8,12},{10,14},{12... | collective-permute-start | bytes 589832 | tf_op jit(solution)/shard_map/ppermute | solution.py:329
  126.0 10.6 %collective-permute-start.23 = (f32[64,768]{1,0:T(8,128)S(1)}, f32[64,768]{1,0:T(8,128)S(1)}, u32[]{:S(2)}, u32[]{:S(2)}) collective-permute-start(f32[64,768]{1,0:T(8,128)S(1)} %get-tuple-element.180), channel_id=1, source_target_pairs={{0,2},{2,0},{4,6},{6,4},{1,3},{3,1},{5,7},{7,5},{8,10},{10,8},{12,... | collective-permute-start | bytes 589832 | tf_op jit(solution)/shard_map/ppermute | solution.py:329
  126.3 4.8 %collective-permute-start.34 = (f32[6,128,128]{2,1,0:T(8,128)S(1)}, f32[6,128,128]{2,1,0:T(8,128)S(1)}, u32[]{:S(2)}, u32[]{:S(2)}) collective-permute-start(f32[6,128,128]{2,1,0:T(8,128)S(1)} %pad_maximum_fusion.6), channel_id=1, source_target_pairs={{0,1},{1,0},{2,3},{3,2},{4,5},{5,4},{6,7},{7,6},{8,9},{9,8},{10,11... | collective-permute-start | bytes 1179656 | tf_op jit(solution)/shard_map/ppermute | solution.py:334
  128.2 9.4 %copy-start = (f32[128,768]{1,0:T(8,128)S(1)}, f32[128,768]{1,0:T(8,128)}, u32[]{:S(2)}) copy-start(f32[128,768]{1,0:T(8,128)} %param.7) | copy-start | bytes 1179652
  128.2 8.9 %collective-permute-start.28 = (f32[32,768]{1,0:T(8,128)S(1)}, f32[32,768]{1,0:T(8,128)S(1)}, u32[]{:S(2)}, u32[]{:S(2)}) collective-permute-start(f32[32,768]{1,0:T(8,128)S(1)} %get-tuple-element.194), channel_id=1, source_target_pairs={{0,6},{2,4},{4,2},{6,0},{1,7},{3,5},{5,3},{7,1},{8,14},{10,12},{12... | collective-permute-start | bytes 294920 | tf_op jit(solution)/shard_map/ppermute | solution.py:329
  131.1 6.5 %collective-permute-start.29 = (f32[32,768]{1,0:T(8,128)S(1)}, f32[32,768]{1,0:T(8,128)S(1)}, u32[]{:S(2)}, u32[]{:S(2)}) collective-permute-start(f32[32,768]{1,0:T(8,128)S(1)} %get-tuple-element.195), channel_id=1, source_target_pairs={{0,4},{2,6},{4,0},{6,2},{1,5},{3,7},{5,1},{7,3},{8,12},{10,14},{12... | collective-permute-start | bytes 294920 | tf_op jit(solution)/shard_map/ppermute | solution.py:329
  133.6 5.6 %collective-permute-start.30 = (f32[32,768]{1,0:T(8,128)S(1)}, f32[32,768]{1,0:T(8,128)S(1)}, u32[]{:S(2)}, u32[]{:S(2)}) collective-permute-start(f32[32,768]{1,0:T(8,128)S(1)} %get-tuple-element.196), channel_id=1, source_target_pairs={{0,2},{2,0},{4,6},{6,4},{1,3},{3,1},{5,7},{7,5},{8,10},{10,8},{12,... | collective-permute-start | bytes 294920 | tf_op jit(solution)/shard_map/ppermute | solution.py:329
  134.0 8.4 %collective-permute-start.35 = (f32[32,768]{1,0:T(8,128)S(1)}, f32[32,768]{1,0:T(8,128)S(1)}, u32[]{:S(2)}, u32[]{:S(2)}) collective-permute-start(f32[32,768]{1,0:T(8,128)S(1)} %get-tuple-element.210), channel_id=1, source_target_pairs={{0,6},{2,4},{4,2},{6,0},{1,7},{3,5},{5,3},{7,1},{8,14},{10,12},{12... | collective-permute-start | bytes 294920 | tf_op jit(solution)/shard_map/ppermute | solution.py:329
  136.6 6.0 %collective-permute-start.36 = (f32[32,768]{1,0:T(8,128)S(1)}, f32[32,768]{1,0:T(8,128)S(1)}, u32[]{:S(2)}, u32[]{:S(2)}) collective-permute-start(f32[32,768]{1,0:T(8,128)S(1)} %get-tuple-element.211), channel_id=1, source_target_pairs={{0,4},{2,6},{4,0},{6,2},{1,5},{3,7},{5,1},{7,3},{8,12},{10,14},{12... | collective-permute-start | bytes 294920 | tf_op jit(solution)/shard_map/ppermute | solution.py:329
  137.1 5.5 %collective-permute-start.37 = (f32[32,768]{1,0:T(8,128)S(1)}, f32[32,768]{1,0:T(8,128)S(1)}, u32[]{:S(2)}, u32[]{:S(2)}) collective-permute-start(f32[32,768]{1,0:T(8,128)S(1)} %get-tuple-element.212), channel_id=1, source_target_pairs={{0,2},{2,0},{4,6},{6,4},{1,3},{3,1},{5,7},{7,5},{8,10},{10,8},{12,... | collective-permute-start | bytes 294920 | tf_op jit(solution)/shard_map/ppermute | solution.py:329
